TPU v7x, 32 devices: a whole 2x2x4 slice. The times are simulated.
32 devices in a mesh: dp: 16 (over z, x, core), tensor: 2 (over y).
Axes of the slice: x: 2, y: 2, z: 4, core: 2. Of those that a mesh axis runs over, the one named last changes fastest.
Arguments:
- tokens: bfloat16 [16384, 1024], P(('dp', 'tensor')), may hold values from -6 to 6
- gain_attn: bfloat16 [1024], P(('dp', 'tensor')), may hold values from 0.5 to 1.5
- gain_ffn: bfloat16 [1024], P(('dp', 'tensor')), may hold values from 0.5 to 1.5
- w_query: bfloat16 [1024, 1024], P('dp', 'tensor'), may hold values from -0.75 to 0.75
- w_key: bfloat16 [1024, 512], P('dp', 'tensor'), may hold values from -0.75 to 0.75
- w_value: bfloat16 [1024, 512], P('dp', 'tensor'), may hold values from -0.1875 to 0.1875
- w_output: bfloat16 [1024, 1024], P('tensor', 'dp'), may hold values from -2 to 2
- w_router: bfloat16 [1024, 16], P(('dp', 'tensor')), may hold values from -0.09375 to 0.09375
- w_gate: bfloat16 [16, 1024, 512], P(None, 'dp', 'tensor'), may hold values from -0.1875 to 0.1875
- w_up: bfloat16 [16, 1024, 512], P(None, 'dp', 'tensor'), may hold values from -0.1875 to 0.1875
- w_down: bfloat16 [16, 512, 1024], P(None, 'tensor', 'dp'), may hold values from -4 to 4
- segments: int32 [16384], P('dp'), may hold values from 0 to 2, as said below
- routes: int32 [16384, 8], P('dp'), may hold values from 0 to 15, all different within a row; in each aligned block of 1024 rows (0 to 1023, 1024 to 2047, ...) at most 640 rows name the same one
- cotangent: bfloat16 [16384, 1024], P(('dp', 'tensor')), may hold values from -6 to 6
Outputs:
- output: float32 [16384, 1024], P(('dp', 'tensor'))
- grad_tokens: float32 [16384, 1024], P(('dp', 'tensor'))
- grad_gain_attn: float32 [1024], P(('dp', 'tensor'))
- grad_gain_ffn: float32 [1024], P(('dp', 'tensor'))
- grad_query: float32 [1024, 1024], P('dp', 'tensor')
- grad_key: float32 [1024, 512], P('dp', 'tensor')
- grad_value: float32 [1024, 512], P('dp', 'tensor')
- grad_output: float32 [1024, 1024], P('tensor', 'dp')
- grad_router: float32 [1024, 16], P(('dp', 'tensor'))
- grad_gate: float32 [16, 1024, 512], P(None, 'dp', 'tensor')
- grad_up: float32 [16, 1024, 512], P(None, 'dp', 'tensor')
- grad_down: float32 [16, 512, 1024], P(None, 'tensor', 'dp')
Inputs may be any that keep to these rules, and one draw needn't show every extreme that they name: `segments`: document numbers restart at 0 in each block of 1024 tokens of one index of dp and never fall within it; each block holds 3 documents. `routes`: within the 1024 tokens of one index of dp, no expert is named by more than 640 tokens.
All inputs are finite; a program needn't handle non-finite values.
Results may differ from a plain program's by a relative error of at most 0.02.
Values may be sent and summed in bfloat16 or wider, within the bound.
A program may use at most 384 MiB of HBM per device.

v0:
```python
import jax
import jax.numpy as jnp
from jax import lax
from jax.sharding import PartitionSpec as P

HEAD = 64
CAP = 640


EPSILON = 1e-06
RESIDUAL_SCALE = 0.22
SCORE_SCALE = 0.015625
MASKED = -1e30
PRECISE = lax.Precision.HIGHEST


def positions(doc_ids):
    index_row = jnp.arange(doc_ids.shape[0], dtype=jnp.int32)
    starting = jnp.concatenate([jnp.ones((1,), dtype=jnp.bool_), doc_ids[1:] != doc_ids[:-1]])
    seg_begin = lax.cummax(jnp.where(starting, index_row, jnp.zeros_like(index_row)), axis=0)
    return index_row - seg_begin


def rotary(places, half_width):
    freqs = 10000.0 ** (-jnp.arange(half_width, dtype=jnp.float32) / half_width)
    angles = places.astype(jnp.float32)[:, None] * freqs[None, :]
    return (jnp.cos(angles)[:, None, :], jnp.sin(angles)[:, None, :])


def rotate(values, cosine, sine):
    half_width = values.shape[-1] // 2
    first_half = values[..., :half_width]
    second_half = values[..., half_width:]
    return jnp.concatenate(
        [first_half * cosine - second_half * sine, second_half * cosine + first_half * sine],
        axis=-1,
    )


def fetch_experts(w_gate, w_up, w_down):
    return (
        lax.all_gather(w_gate, "dp", axis=1, tiled=True),
        lax.all_gather(w_up, "dp", axis=1, tiled=True),
        lax.all_gather(w_down, "dp", axis=2, tiled=True),
    )


def norm_back(grad_normed, base, inverse, gain):
    grad_gain = jnp.sum(grad_normed * base, axis=0)
    scaled = grad_normed * gain
    grad_in = inverse * scaled - base * inverse * jnp.mean(scaled * base, axis=-1, keepdims=True)
    return (grad_in, grad_gain)


def on_device(
    tokens,
    gain_attn,
    gain_ffn,
    w_query,
    w_key,
    w_value,
    w_output,
    w_router,
    w_gate,
    w_up,
    w_down,
    segments,
    routes,
    cotangent,
):
    gain_one, gain_two, router = (
        lax.all_gather(gain_attn, ("dp", "tensor"), axis=0, tiled=True),
        lax.all_gather(gain_ffn, ("dp", "tensor"), axis=0, tiled=True),
        lax.all_gather(w_router, ("dp", "tensor"), axis=0, tiled=True),
    )
    query_w, key_w, value_w, out_w = (
        lax.all_gather(w_query, "dp", axis=0, tiled=True),
        lax.all_gather(w_key, "dp", axis=0, tiled=True),
        lax.all_gather(w_value, "dp", axis=0, tiled=True),
        lax.all_gather(w_output, "dp", axis=1, tiled=True),
    )
    gate_w, up_w, down_w = fetch_experts(w_gate, w_up, w_down)
    total = segments.shape[0]
    width = tokens.shape[1]
    heads_here = query_w.shape[1] // HEAD
    groups_here = key_w.shape[1] // HEAD
    repeat = heads_here // groups_here
    experts = w_gate.shape[0]
    top_count = routes.shape[1]
    capacity = CAP
    gain_one = gain_one.astype(jnp.float32)
    gain_two = gain_two.astype(jnp.float32)
    cosine, sine = rotary(positions(segments), HEAD // 2)
    index_row = jnp.arange(total, dtype=jnp.int32)
    allowed = (segments[:, None] == segments[None, :]) & (index_row[None, :] <= index_row[:, None])
    inputs = tokens.astype(jnp.float32)
    inverse_one = lax.rsqrt(jnp.mean(inputs * inputs, axis=-1, keepdims=True) + EPSILON)
    base_one = inputs * inverse_one
    normed_one = (base_one * gain_one).astype(jnp.bfloat16)
    rows_one = lax.all_gather(normed_one, "tensor", axis=0, tiled=True)
    query_lin = jnp.dot(rows_one, query_w, preferred_element_type=jnp.float32).reshape(
        total, heads_here, HEAD
    )
    key_lin = jnp.dot(rows_one, key_w, preferred_element_type=jnp.float32).reshape(
        total, groups_here, HEAD
    )
    values = (
        jnp.dot(rows_one, value_w, preferred_element_type=jnp.float32)
        .astype(jnp.bfloat16)
        .reshape(total, groups_here, HEAD)
    )
    queries = (
        rotate(query_lin, cosine, sine)
        .astype(jnp.bfloat16)
        .reshape(total, groups_here, repeat, HEAD)
    )
    keys = rotate(key_lin, cosine, sine).astype(jnp.bfloat16)

    def score_block():
        raw = (
            jnp.einsum("igrd,jgd->grij", queries, keys, preferred_element_type=jnp.float32)
            * SCORE_SCALE
        )
        return jnp.where(allowed, raw, MASKED)

    scores = score_block()
    top_score = jnp.max(scores, axis=-1, keepdims=True)
    expo = jnp.exp(scores - top_score)
    denom = jnp.sum(expo, axis=-1, keepdims=True)
    log_total = top_score + jnp.log(denom)
    probs = expo / denom
    mixed = jnp.einsum(
        "grij,jgd->igrd", probs.astype(jnp.bfloat16), values, preferred_element_type=jnp.float32
    )
    mixed = mixed.reshape(total, heads_here * HEAD).astype(jnp.bfloat16)
    attn_part = jnp.dot(mixed, out_w, preferred_element_type=jnp.float32)
    attn_total = lax.psum_scatter(attn_part, "tensor", scatter_dimension=0, tiled=True)
    after_attn = inputs + RESIDUAL_SCALE * attn_total
    inverse_two = lax.rsqrt(jnp.mean(after_attn * after_attn, axis=-1, keepdims=True) + EPSILON)
    base_two = after_attn * inverse_two
    normed_two = (base_two * gain_two).astype(jnp.bfloat16)
    rows_two = lax.all_gather(normed_two, "tensor", axis=0, tiled=True)
    logits = jnp.dot(rows_two, router, preferred_element_type=jnp.float32)
    expert_ids = jnp.arange(experts, dtype=jnp.int32)
    onehot = (routes[:, :, None] == expert_ids[None, None, :]).astype(jnp.float32)
    chosen = jnp.einsum("tke,te->tk", onehot, logits, precision=PRECISE)
    gates = jax.nn.softmax(chosen, axis=-1)
    flat_ids = routes.reshape(total * top_count)
    picked = (flat_ids[:, None] == expert_ids[None, :]).astype(jnp.int32)
    ranks = jnp.sum(picked * (jnp.cumsum(picked, axis=0) - 1), axis=1)
    slot_of = flat_ids * capacity + ranks
    owner = (
        jnp.zeros((experts * capacity,), jnp.int32)
        .at[slot_of]
        .set(jnp.arange(total * top_count, dtype=jnp.int32) // top_count)
    )
    slot_gate = (
        jnp.zeros((experts * capacity,), jnp.float32)
        .at[slot_of]
        .set(gates.reshape(total * top_count))
    )
    in_buffer = rows_two[owner].reshape(experts, capacity, width)
    gate_pre = jnp.einsum("ecd,edf->ecf", in_buffer, gate_w, preferred_element_type=jnp.float32)
    up_pre = jnp.einsum("ecd,edf->ecf", in_buffer, up_w, preferred_element_type=jnp.float32)
    sigmoid_gate = jax.nn.sigmoid(gate_pre)
    activated = gate_pre * sigmoid_gate
    hidden = (activated * up_pre).astype(jnp.bfloat16)
    out_buffer = jnp.einsum(
        "ecf,efd->ecd", hidden, down_w, preferred_element_type=jnp.float32
    ).reshape(experts * capacity, width)
    per_route = out_buffer[slot_of].reshape(total, top_count, width)
    moe_part = jnp.sum(gates[:, :, None] * per_route, axis=1)
    moe_total = lax.psum_scatter(
        moe_part.astype(jnp.bfloat16), "tensor", scatter_dimension=0, tiled=True
    ).astype(jnp.float32)
    output = after_attn + RESIDUAL_SCALE * moe_total
    grad_out = cotangent.astype(jnp.float32)
    moe_grad = (RESIDUAL_SCALE * grad_out).astype(jnp.bfloat16)
    moe_grad_rows = lax.all_gather(moe_grad, "tensor", axis=0, tiled=True)
    grad_gates = jnp.sum(moe_grad_rows.astype(jnp.float32)[:, None, :] * per_route, axis=-1)
    grad_buffer = (
        (slot_gate[:, None] * moe_grad_rows[owner].astype(jnp.float32))
        .astype(jnp.bfloat16)
        .reshape(experts, capacity, width)
    )
    gate_w, up_w, down_w = fetch_experts(w_gate, w_up, w_down)
    grad_hidden = jnp.einsum(
        "ecd,efd->ecf", grad_buffer, down_w, preferred_element_type=jnp.float32
    )
    grad_gate_pre = (
        grad_hidden * up_pre * sigmoid_gate * (1.0 + gate_pre * (1.0 - sigmoid_gate))
    ).astype(jnp.bfloat16)
    grad_up_pre = (grad_hidden * activated).astype(jnp.bfloat16)
    grad_down_w = jnp.einsum(
        "ecf,ecd->efd", hidden, grad_buffer, preferred_element_type=jnp.float32
    )
    grad_gate_w = jnp.einsum(
        "ecd,ecf->edf", in_buffer, grad_gate_pre, preferred_element_type=jnp.float32
    )
    grad_up_w = jnp.einsum(
        "ecd,ecf->edf", in_buffer, grad_up_pre, preferred_element_type=jnp.float32
    )
    grad_in_buffer = jnp.einsum(
        "ecf,edf->ecd", grad_gate_pre, gate_w, preferred_element_type=jnp.float32
    )
    grad_in_buffer = grad_in_buffer + jnp.einsum(
        "ecf,edf->ecd", grad_up_pre, up_w, preferred_element_type=jnp.float32
    )
    grad_gate, grad_up, grad_down = (
        lax.psum_scatter(grad_gate_w, "dp", scatter_dimension=1, tiled=True),
        lax.psum_scatter(grad_up_w, "dp", scatter_dimension=1, tiled=True),
        lax.psum_scatter(grad_down_w, "dp", scatter_dimension=2, tiled=True),
    )
    grad_rows_two = jnp.sum(
        grad_in_buffer.reshape(experts * capacity, width)[slot_of].reshape(total, top_count, width),
        axis=1,
    )
    grad_select = gates * (grad_gates - jnp.sum(gates * grad_gates, axis=-1, keepdims=True))
    grad_logits = jnp.einsum("tk,tke->te", grad_select, onehot, precision=PRECISE)
    router_f = router.astype(jnp.float32)
    grad_router_w = jnp.dot(rows_two.astype(jnp.float32).T, grad_logits, precision=PRECISE)
    grad_rows_two = grad_rows_two + jnp.dot(grad_logits, router_f.T, precision=PRECISE)
    grad_normed_two = lax.psum_scatter(
        grad_rows_two.astype(jnp.bfloat16), "tensor", scatter_dimension=0, tiled=True
    ).astype(jnp.float32)
    grad_in_two, grad_gain_two = norm_back(grad_normed_two, base_two, inverse_two, gain_two)
    grad_after = grad_out + grad_in_two
    attn_grad = (RESIDUAL_SCALE * grad_after).astype(jnp.bfloat16)
    attn_grad_rows = lax.all_gather(attn_grad, "tensor", axis=0, tiled=True)
    grad_out_w = jnp.dot(mixed.T, attn_grad_rows, preferred_element_type=jnp.float32)
    grad_mixed = jnp.dot(attn_grad_rows, out_w.T, preferred_element_type=jnp.float32).astype(
        jnp.bfloat16
    )
    grad_mixed = grad_mixed.reshape(total, groups_here, repeat, HEAD)
    probs_again = jnp.exp(score_block() - log_total)
    grad_probs = jnp.einsum(
        "igrd,jgd->grij", grad_mixed, values, preferred_element_type=jnp.float32
    )
    row_delta = jnp.sum(probs_again * grad_probs, axis=-1, keepdims=True)
    grad_scores = (probs_again * (grad_probs - row_delta) * SCORE_SCALE).astype(jnp.bfloat16)
    grad_query_rot = jnp.einsum(
        "grij,jgd->igrd", grad_scores, keys, preferred_element_type=jnp.float32
    ).reshape(total, heads_here, HEAD)
    grad_key_rot = jnp.einsum(
        "grij,igrd->jgd", grad_scores, queries, preferred_element_type=jnp.float32
    )
    grad_values = jnp.einsum(
        "grij,igrd->jgd",
        probs_again.astype(jnp.bfloat16),
        grad_mixed,
        preferred_element_type=jnp.float32,
    )
    grad_values = grad_values.astype(jnp.bfloat16).reshape(total, groups_here * HEAD)
    grad_query_lin = (
        rotate(grad_query_rot, cosine, -sine).astype(jnp.bfloat16).reshape(total, heads_here * HEAD)
    )
    grad_key_lin = (
        rotate(grad_key_rot, cosine, -sine).astype(jnp.bfloat16).reshape(total, groups_here * HEAD)
    )
    grad_query_w = jnp.dot(rows_one.T, grad_query_lin, preferred_element_type=jnp.float32)
    grad_key_w = jnp.dot(rows_one.T, grad_key_lin, preferred_element_type=jnp.float32)
    grad_value_w = jnp.dot(rows_one.T, grad_values, preferred_element_type=jnp.float32)
    grad_rows_one = jnp.dot(grad_query_lin, query_w.T, preferred_element_type=jnp.float32)
    grad_rows_one = grad_rows_one + jnp.dot(
        grad_key_lin, key_w.T, preferred_element_type=jnp.float32
    )
    grad_rows_one = grad_rows_one + jnp.dot(
        grad_values, value_w.T, preferred_element_type=jnp.float32
    )
    grad_normed_one = lax.psum_scatter(
        grad_rows_one.astype(jnp.bfloat16), "tensor", scatter_dimension=0, tiled=True
    ).astype(jnp.float32)
    grad_in_one, grad_gain_one = norm_back(grad_normed_one, base_one, inverse_one, gain_one)
    grad_tokens = grad_after + grad_in_one
    grad_query, grad_key, grad_value, grad_output = (
        lax.psum_scatter(grad_query_w, "dp", scatter_dimension=0, tiled=True),
        lax.psum_scatter(grad_key_w, "dp", scatter_dimension=0, tiled=True),
        lax.psum_scatter(grad_value_w, "dp", scatter_dimension=0, tiled=True),
        lax.psum_scatter(grad_out_w, "dp", scatter_dimension=1, tiled=True),
    )
    grad_gain_attn, grad_gain_ffn, grad_router = (
        lax.psum_scatter(grad_gain_one, ("dp", "tensor"), scatter_dimension=0, tiled=True),
        lax.psum_scatter(grad_gain_two, ("dp", "tensor"), scatter_dimension=0, tiled=True),
        lax.psum_scatter(grad_router_w, ("dp", "tensor"), scatter_dimension=0, tiled=True),
    )
    return (
        output,
        grad_tokens,
        grad_gain_attn,
        grad_gain_ffn,
        grad_query,
        grad_key,
        grad_value,
        grad_output,
        grad_router,
        grad_gate,
        grad_up,
        grad_down,
    )


def solution(mesh):
    in_specs = (
        P(("dp", "tensor"), None),
        P(("dp", "tensor")),
        P(("dp", "tensor")),
        P("dp", "tensor"),
        P("dp", "tensor"),
        P("dp", "tensor"),
        P("tensor", "dp"),
        P(("dp", "tensor"), None),
        P(None, "dp", "tensor"),
        P(None, "dp", "tensor"),
        P(None, "tensor", "dp"),
        P("dp"),
        P("dp", None),
        P(("dp", "tensor"), None),
    )
    out_specs = (
        P(("dp", "tensor"), None),
        P(("dp", "tensor"), None),
        P(("dp", "tensor")),
        P(("dp", "tensor")),
        P("dp", "tensor"),
        P("dp", "tensor"),
        P("dp", "tensor"),
        P("tensor", "dp"),
        P(("dp", "tensor"), None),
        P(None, "dp", "tensor"),
        P(None, "dp", "tensor"),
        P(None, "tensor", "dp"),
    )
    return jax.shard_map(
        on_device, mesh=mesh, in_specs=in_specs, out_specs=out_specs, check_vma=False
    )
```

profile of v0, /device:TPU:0, one launch (start us, length us, event | category | flops | bytes accessed | tf_op | source)
XLA Modules:
  0.0 1885.8 jit_solution(3072124980133862063)
XLA Ops:
  10.4 42.0 %all-reduce.5 = (bf16[1024]{0:T(1024)(128)(2,1)S(1)}, bf16[1024]{0:T(1024)(128)(2,1)S(1)}) all-reduce(bf16[1024]{0:T(1024)(128)(2,1)S(1)} %dynamic-update-slice, bf16[1024]{0:T(1024)(128)(2,1)S(1)} %dynamic-update-slice.1), channel_id=1, replica_groups=mesh['dp'=16,'tensor'=2] {'dp','tensor'}, use_global_device_ids=true, to_apply=%add | all-reduce | flops 2048 | bytes 8192
  60.0 22.8 %all_gather.48 = bf16[1024,256]{1,0:T(8,128)(2,1)S(1)} all-gather(bf16[64,256]{1,0:T(8,128)(2,1)} %param.18), channel_id=1, replica_groups=mesh['dp'=16,'tensor'=2] {'dp'}, dimensions={0}, use_global_device_ids=true | all-gather | bytes 557056 | tf_op jit(solution)/shard_map/all_gather | solution.py:78
  82.8 19.3 %all_gather.47 = bf16[1024,256]{1,0:T(8,128)(2,1)S(1)} all-gather(bf16[64,256]{1,0:T(8,128)(2,1)} %param.19), channel_id=1, replica_groups=mesh['dp'=16,'tensor'=2] {'dp'}, dimensions={0}, use_global_device_ids=true | all-gather | bytes 557056 | tf_op jit(solution)/shard_map/all_gather | solution.py:79
  105.8 23.0 %all-gather.13.cloned.1.call-done = bf16[1024,512]{1,0:T(8,128)(2,1)} async-done(((bf16[64,512]{1,0:T(8,128)(2,1)}), bf16[1024,512]{1,0:T(8,128)(2,1)}) %all-gather.13.cloned.1.call-update) | async-done | bytes 1048592 | tf_op jit(solution)/shard_map/all_gather | solution.py:77
  132.3 13.6 fusion.12
  146.0 14.4 fusion.6
  162.1 15.5 fusion.38
  177.6 4.9 fusion.81
  184.1 51.9 %reduce-scatter.15.cloned.1.call-done = f32[512,1024]{1,0:T(8,128)} async-done(((f32[1024,1024]{1,0:T(8,128)}), f32[512,1024]{1,0:T(8,128)}) %reduce-scatter.15.cloned.1.call-update) | async-done | bytes 2097168 | tf_op jit(solution)/shard_map/reduce_scatter | solution.py:137
  243.6 68.7 %all-gather = bf16[32,32,16]{1,2,0:T(8,128)(2,1)S(1)} all-gather(bf16[1,32,16]{1,2,0:T(8,128)(2,1)S(1)} %bitcast.244), channel_id=1, replica_groups=mesh['dp'=16,'tensor'=2] {'dp','tensor'}, dimensions={0}, use_global_device_ids=true | all-gather | bytes 33792 | tf_op jit(solution)/shard_map/all_gather | solution.py:74
  313.2 4.8 reduce-window.19
  321.7 30.5 %scatter_custom_fusion = s32[10240]{0:T(1024)S(1)} fusion(s32[8192]{0:T(1024)S(1)} %bitcast.235, s32[8192]{0:T(1024)S(1)} %add_select_fusion, s32[]{:T(128)} %constant.52.clone.1), kind=kCustom, calls=%fused_computation.123 | custom fusion | bytes 40964 | tf_op jit(solution)/shard_map/scatter | solution.py:155
  352.9 52.4 %gather_fusion.2 = bf16[10240,1024]{1,0:T(8,128)(2,1)} fusion(bf16[1024,1024]{1,0:T(8,128)(2,1)} %all-gather.25.cloned.1.call-done, s32[10240]{0:T(1024)S(1)} %fusion.52), kind=kCustom, calls=%fused_computation.2 | custom fusion | bytes 41984000 | tf_op jit(solution)/shard_map/gather | solution.py:182
  405.3 30.8 %copy.66 = f32[16,640,1024]{1,2,0:T(8,128)} copy(bf16[16,640,1024]{2,1,0:T(8,128)(2,1)} %bitcast.212) | data formatting | bytes 62914560 | tf_op jit(solution)/shard_map/convert_element_type | solution.py:182
  442.4 30.9 %scatter_custom_fusion.1 = f32[10240]{0:T(1024)S(1)} fusion(s32[8192]{0:T(1024)S(1)} %bitcast.237, f32[8192]{0:T(1024)S(1)} %reshape.351, f32[]{:T(128)} %constant.21.clone.1), kind=kCustom, calls=%fused_computation.121 | custom fusion | bytes 40964 | tf_op jit(solution)/shard_map/scatter | solution.py:160
  473.3 44.1 %gather_fusion = bf16[10240,1024]{1,0:T(8,128)(2,1)} fusion(bf16[1024,1024]{1,0:T(8,128)(2,1)S(1)} %copy-done, s32[10240]{0:T(1024)S(1)} %fusion.52), kind=kCustom, calls=%fused_computation | custom fusion | bytes 41984000 | tf_op jit(solution)/shard_map/gather | solution.py:162
  517.4 14.9 fusion.84
  532.3 14.8 fusion.83
  547.1 30.0 %multiply_convert_fusion.1 = (bf16[16,640,256]{2,1,0:T(8,128)(2,1)}, bf16[16,640,256]{2,1,0:T(8,128)(2,1)}, bf16[16,640,256]{2,1,0:T(8,128)(2,1)}) fusion(f32[16,640,256]{2,1,0:T(8,128)} %fusion.83, f32[16,640,256]{2,1,0:T(8,128)} %fusion.84, bf16[16,256,1024]{1,2,0:T(8,128)(2,1)} %all-gather.23.cloned.1.call-done, f32[16,640,1024]{1,2,0:T(8,128)} %copy.66, ...), kind=kOutput, calls=%fused_computation.32 | convolution fusion | flops 5429002240 | bytes 87072768 | tf_op jit(solution)/shard_map/ecd,efd->ecf/dot_general | solution.py:187
  577.1 20.4 %fusion.86 = f32[16,640,1024]{2,1,0:T(8,128)} fusion(bf16[16,640,256]{2,1,0:T(8,128)(2,1)} %get-tuple-element.25, bf16[16,1024,256]{2,1,0:T(8,128)(2,1)} %all-gather.19.cloned.1.call-done), kind=kOutput, calls=%fused_computation.158 | convolution fusion | flops 5368709120 | bytes 55574528 | tf_op jit(solution)/shard_map/ecf,edf->ecd/dot_general | solution.py:203
  597.4 32.7 %convolution_add_fusion = f32[16,640,1024]{2,1,0:T(8,128)} fusion(f32[16,640,1024]{2,1,0:T(8,128)} %fusion.86, bf16[16,640,256]{2,1,0:T(8,128)(2,1)} %get-tuple-element.24, bf16[16,1024,256]{2,1,0:T(8,128)(2,1)} %all-gather.21.cloned.1.call-done), kind=kOutput, calls=%fused_computation.27 | convolution fusion | flops 5379194880 | bytes 97517568 | tf_op jit(solution)/shard_map/ecf,edf->ecd/dot_general | solution.py:206
  630.1 56.8 %gather_fusion.3 = f32[8192,1024]{1,0:T(8,128)} fusion(f32[10240,1024]{1,0:T(8,128)} %bitcast.207, s32[8192]{0:T(1024)S(1)} %copy-done.40), kind=kCustom, calls=%fused_computation.3 | custom fusion | bytes 67141632 | tf_op jit(solution)/shard_map/gather | solution.py:215
  686.9 16.9 bitcast_reduce_fusion
  703.9 20.4 %fusion.85 = f32[16,640,1024]{2,1,0:T(8,128)} fusion(bf16[16,640,256]{2,1,0:T(8,128)(2,1)} %get-tuple-element.26, bf16[16,256,1024]{1,2,0:T(8,128)(2,1)} %all-gather.23.cloned.1.call-done), kind=kOutput, calls=%fused_computation.157 | convolution fusion | flops 5368709120 | bytes 55574528 | tf_op jit(solution)/shard_map/ecf,efd->ecd/dot_general | solution.py:168
  724.2 56.7 %gather_fusion.1 = f32[8192,1024]{1,0:T(8,128)} fusion(f32[10240,1024]{1,0:T(8,128)} %bitcast.206, s32[8192]{0:T(1024)S(1)} %copy-done.40), kind=kCustom, calls=%fused_computation.1 | custom fusion | bytes 67141632 | tf_op jit(solution)/shard_map/gather | solution.py:171
  780.9 17.3 fusion.5
  799.2 5.1 fusion.87
  808.6 27.8 %reduce-scatter.19.cloned.1.call-done = bf16[512,1024]{1,0:T(8,128)(2,1)} async-done(((bf16[1024,1024]{1,0:T(8,128)(2,1)}), bf16[512,1024]{1,0:T(8,128)(2,1)}) %reduce-scatter.19.cloned.1.call-update) | async-done | bytes 1048592 | tf_op jit(solution)/shard_map/reduce_scatter | solution.py:223
  839.6 3.6 multiply_convert_fusion.6
  843.3 4.2 fusion.95
  847.6 28.9 %all-gather.27.cloned.1.call-done = bf16[1024,1024]{1,0:T(8,128)(2,1)} async-done(((bf16[512,1024]{1,0:T(8,128)(2,1)}), bf16[1024,1024]{1,0:T(8,128)(2,1)}) %all-gather.27.cloned.1.call-update) | async-done | bytes 2097168 | tf_op jit(solution)/shard_map/all_gather | solution.py:229
  879.7 13.6 fusion.88
  893.3 15.0 fusion.43
  908.3 46.2 %fusion.39 = f32[1024,4,64]{0,2,1:T(8,128)} fusion(f32[4,1024,1024,2]{2,1,3,0:T(8,128)} %fusion.88, f32[4,2,1024]{2,1,0:T(2,128)S(1)} %bitcast.242, f32[4,1024,1024,2]{2,1,3,0:T(8,128)} %get-tuple-element.41, pred[1024,1024]{0,1:T(8,128)(4,1)S(1)} %copy-done.19, bf16[1024,4,2,32]{0,3,2,1:T(8,128)(2,1)} %bitcast.233, bf16[1024,4,2,32]{0,3,2,1:T(8,128)(2,1)S(1)} %bitcast.231), kind=kOutput, calls=%fused_computation.75 | convolution fusion | flops 1168122880 | bytes 70287360 | tf_op jit(solution)/shard_map/grij,igrd->jgd/dot_general | solution.py:244
  954.5 45.9 %fusion.15 = f32[4,64,2,1024]{3,1,2,0:T(8,128)} fusion(f32[4,1024,1024,2]{2,1,3,0:T(8,128)} %fusion.88, f32[4,2,1024]{2,1,0:T(2,128)S(1)} %bitcast.243, f32[4,1024,1024,2]{2,1,3,0:T(8,128)} %get-tuple-element.41, pred[1024,1024]{0,1:T(8,128)(4,1)S(1)} %copy-done.19, bf16[1024,4,32]{0,2,1:T(8,128)(2,1)S(1)} %copy-done.44, bf16[1024,4,32]{0,2,1:T(8,128)(2,1)S(1)} %copy-done.42), kind=kOutput, calls=%fused_computation.31 | convolution fusion | flops 1167074304 | bytes 70811648 | tf_op jit(solution)/shard_map/grij,jgd->igrd/dot_general | solution.py:241
  1012.1 4.7 fusion.94
  1019.6 23.9 %fusion.17 = f32[16,256,1024]{1,2,0:T(8,128)} fusion(bf16[16,640,256]{2,1,0:T(8,128)(2,1)} %get-tuple-element.26, f32[16,640,1024]{1,2,0:T(8,128)} %copy.66, f32[16,640]{1,0:T(8,128)S(1)} %copy-done.37), kind=kOutput, calls=%fused_computation.37 | convolution fusion | flops 5389680640 | bytes 64004096 | tf_op jit(solution)/shard_map/ecf,ecd->efd/dot_general | solution.py:194
  1043.6 18.8 fusion.96
  1062.5 18.7 fusion.97
  1084.9 39.7 %all-reduce.4 = (f32[1024]{0:T(1024)S(1)}, f32[1024]{0:T(1024)S(1)}) all-reduce(f32[1024]{0:T(1024)S(1)} %get-tuple-element.16, f32[1024]{0:T(1024)S(1)} %copy-done.65), channel_id=6, replica_groups=mesh['dp'=16,'tensor'=2] {'dp','tensor'}, use_global_device_ids=true, to_apply=%region_25.26.clone | all-reduce | flops 2048 | bytes 16384
  1125.8 4.4 fusion.28
  1130.2 9.6 reduce-scatter.27.cloned.1.call-done
  1139.8 60.5 %reduce-scatter.25.cloned.1.call-done = f32[64,256]{1,0:T(8,128)} async-done(((f32[1024,256]{1,0:T(8,128)}), f32[64,256]{1,0:T(8,128)}) %reduce-scatter.25.cloned.1.call-update) | async-done | bytes 65552 | tf_op jit(solution)/shard_map/reduce_scatter | solution.py:277
  1200.3 65.2 %reduce-scatter.29.cloned.1.call-done = f32[512,64]{0,1:T(8,128)} async-done(((f32[512,1024]{0,1:T(8,128)}), f32[512,64]{0,1:T(8,128)}) %reduce-scatter.29.cloned.1.call-update) | async-done | bytes 131088 | tf_op jit(solution)/shard_map/reduce_scatter | solution.py:279
  1265.5 64.9 %reduce-scatter.23.cloned.1.call-done = f32[64,512]{1,0:T(8,128)} async-done(((f32[1024,512]{1,0:T(8,128)}), f32[64,512]{1,0:T(8,128)}) %reduce-scatter.23.cloned.1.call-update) | async-done | bytes 131088 | tf_op jit(solution)/shard_map/reduce_scatter | solution.py:276
  1330.4 182.8 %reduce-scatter.35.cloned.1.call-done = f32[16,256,64]{1,2,0:T(8,128)} async-done(((f32[16,256,1024]{1,2,0:T(8,128)}), f32[16,256,64]{1,2,0:T(8,128)}) %reduce-scatter.35.cloned.1.call-update) | async-done | bytes 1048592 | tf_op jit(solution)/shard_map/reduce_scatter | solution.py:212
  1513.2 182.7 %reduce-scatter.31.cloned.1.call-done = f32[16,64,256]{2,1,0:T(8,128)} async-done(((f32[16,1024,256]{2,1,0:T(8,128)}), f32[16,64,256]{2,1,0:T(8,128)}) %reduce-scatter.31.cloned.1.call-update) | async-done | bytes 1048592 | tf_op jit(solution)/shard_map/reduce_scatter | solution.py:210
  1695.9 182.9 %reduce-scatter.33.cloned.1.call-done = f32[16,64,256]{2,1,0:T(8,128)} async-done(((f32[16,1024,256]{2,1,0:T(8,128)}), f32[16,64,256]{2,1,0:T(8,128)}) %reduce-scatter.33.cloned.1.call-update) | async-done | bytes 1048592 | tf_op jit(solution)/shard_map/reduce_scatter | solution.py:211
  (264 shorter events, 70.9 us)
Async XLA Ops:
  7.2 96.1 %all-gather.11.cloned.1.call-start = ((), (), s32[]{:S(2)}) async-start(), calls=%async_computation.12 | async-start | bytes 3145728 | tf_op jit(solution)/shard_map/all_gather | solution.py:100
  8.7 50.6 %copy-start.61 = (f32[512]{0:T(512)}, f32[512]{0:T(512)S(1)}, u32[]{:S(2)}) copy-start(f32[512]{0:T(512)S(1)} %add_rsqrt_fusion.1) | copy-start | bytes 6148
  55.6 73.2 %all-gather.13.cloned.1.call-start = ((), (), s32[]{:S(2)}) async-start(), calls=%async_computation.13 | async-start | bytes 1114112 | tf_op jit(solution)/shard_map/all_gather | solution.py:77
  56.3 121.2 %all-gather.15.cloned.1.call-start = ((), (), s32[]{:S(2)}) async-start(), calls=%async_computation.14 | async-start | bytes 1114112 | tf_op jit(solution)/shard_map/all_gather | solution.py:80
  57.1 179.0 %reduce-scatter.15.cloned.1.call-start = ((), (), s32[]{:S(2)}) async-start(), calls=%async_computation.15 | async-start | bytes 6291456 | tf_op jit(solution)/shard_map/reduce_scatter | solution.py:137
  59.3 101.9 %copy-start.18 = (pred[1024,1024]{0,1:T(8,128)(4,1)}, pred[1024,1024]{0,1:T(8,128)(4,1)S(1)}, u32[]{:S(2)}) copy-start(pred[1024,1024]{0,1:T(8,128)(4,1)S(1)} %fusion.19) | copy-start | bytes 3145732
  82.8 49.5 %copy-start.16 = (bf16[1024,256]{1,0:T(8,128)(2,1)}, bf16[1024,256]{1,0:T(8,128)(2,1)S(1)}, u32[]{:S(2)}) copy-start(bf16[1024,256]{1,0:T(8,128)(2,1)S(1)} %all_gather.48) | copy-start | bytes 1572868
  102.1 58.4 %copy-start.24 = (bf16[1024,256]{1,0:T(8,128)(2,1)}, bf16[1024,256]{1,0:T(8,128)(2,1)S(1)}, u32[]{:S(2)}) copy-start(bf16[1024,256]{1,0:T(8,128)(2,1)S(1)} %all_gather.47) | copy-start | bytes 1572868
  103.2 42.7 %copy-start.22 = (f32[1024,32]{0,1:T(8,128)}, f32[1024,32]{0,1:T(8,128)S(1)}, u32[]{:S(2)}) copy-start(f32[1024,32]{0,1:T(8,128)S(1)} %get-tuple-element.39) | copy-start | bytes 393220
  105.8 40.1 %copy-start.41 = (bf16[1024,4,32]{0,2,1:T(8,128)(2,1)}, bf16[1024,4,32]{0,2,1:T(8,128)(2,1)S(1)}, u32[]{:S(2)}) copy-start(bf16[1024,4,32]{0,2,1:T(8,128)(2,1)S(1)} %get-tuple-element.35) | copy-start | bytes 786436
  105.8 40.1 %copy-start.43 = (bf16[1024,4,32]{0,2,1:T(8,128)(2,1)}, bf16[1024,4,32]{0,2,1:T(8,128)(2,1)S(1)}, u32[]{:S(2)}) copy-start(bf16[1024,4,32]{0,2,1:T(8,128)(2,1)S(1)} %get-tuple-element.36) | copy-start | bytes 786436
  177.6 58.5 %copy-start.7 = (bf16[512,1024]{1,0:T(8,128)(2,1)S(1)}, bf16[512,1024]{1,0:T(8,128)(2,1)}, u32[]{:S(2)}) copy-start(bf16[512,1024]{1,0:T(8,128)(2,1)} %param.14) | copy-start | bytes 3145732
  182.5 60.4 %copy-start.32 = (s32[1024,8]{0,1:T(8,128)S(1)}, s32[1024,8]{0,1:T(8,128)}, u32[]{:S(2)}) copy-start(s32[1024,8]{0,1:T(8,128)} %param.26) | copy-start | bytes 98308
  182.5 61.1 %copy-start.66 = (bf16[32,16]{0,1:T(8,128)(2,1)S(1)}, bf16[32,16]{0,1:T(8,128)(2,1)}, u32[]{:S(2)}) copy-start(bf16[32,16]{0,1:T(8,128)(2,1)} %param.21) | copy-start | bytes 3076
  182.5 170.3 %all-gather.25.cloned.1.call-start = ((), (), s32[]{:S(2)}) async-start(), calls=%async_computation.21 | async-start | bytes 3145728 | tf_op jit(solution)/shard_map/all_gather | solution.py:179
  183.8 254.8 %all-gather.17.cloned.1.call-start = ((), (), s32[]{:S(2)}) async-start(), calls=%async_computation.16 | async-start | bytes 3145728 | tf_op jit(solution)/shard_map/all_gather | solution.py:142
  184.1 59.0 %copy-start.49 = (f32[1024]{0:T(1024)}, f32[1024]{0:T(1024)S(1)}, u32[]{:S(2)}) copy-start(f32[1024]{0:T(1024)S(1)} %convert_element_type.132) | copy-start | bytes 12292
  240.6 276.8 %all-gather.21.cloned.1.call-start = ((), (), s32[]{:S(2)}) async-start(), calls=%async_computation.18 | async-start | bytes 8912896 | tf_op jit(solution)/shard_map/all_gather | solution.py:43
  241.3 291.0 %all-gather.19.cloned.1.call-start = ((), (), s32[]{:S(2)}) async-start(), calls=%async_computation.17 | async-start | bytes 8912896 | tf_op jit(solution)/shard_map/all_gather | solution.py:42
  242.1 305.0 %all-gather.23.cloned.1.call-start = ((), (), s32[]{:S(2)}) async-start(), calls=%async_computation.19 | async-start | bytes 8912896 | tf_op jit(solution)/shard_map/all_gather | solution.py:44
  242.8 593.6 %reduce-scatter.19.cloned.1.call-start = ((), (), s32[]{:S(2)}) async-start(), calls=%async_computation.22 | async-start | bytes 3145728 | tf_op jit(solution)/shard_map/reduce_scatter | solution.py:223
  312.6 126.0 %copy-start.38 = (bf16[1024,16]{0,1:T(8,128)(2,1)}, bf16[1024,16]{0,1:T(8,128)(2,1)S(1)}, u32[]{:S(2)}) copy-start(bf16[1024,16]{0,1:T(8,128)(2,1)S(1)} %reshape.362) | copy-start | bytes 98308
  441.3 76.0 %copy-start.10 = (f32[1024,8]{1,0:T(8,128)}, f32[1024,8]{1,0:T(8,128)S(1)}, u32[]{:S(2)}) copy-start(f32[1024,8]{1,0:T(8,128)S(1)} %copy.81) | copy-start | bytes 98308
  442.1 75.3 %copy-start.14 = (f32[1024,8]{1,0:T(8,128)}, f32[1024,8]{1,0:T(8,128)S(1)}, u32[]{:S(2)}) copy-start(f32[1024,8]{1,0:T(8,128)S(1)} %fusion.50) | copy-start | bytes 98308
  473.3 73.8 %copy-start.36 = (f32[16,640]{1,0:T(8,128)}, f32[16,640]{1,0:T(8,128)S(1)}, u32[]{:S(2)}) copy-start(f32[16,640]{1,0:T(8,128)S(1)} %mul.375) | copy-start | bytes 122884
  724.2 56.7 %copy-start.15 = (f32[1024,8]{1,0:T(8,128)S(1)}, f32[1024,8]{1,0:T(8,128)}, u32[]{:S(2)}) copy-start(f32[1024,8]{1,0:T(8,128)} %copy-done.14) | copy-start | bytes 98308
  799.2 40.4 %copy-start.13 = (bf16[512,1024]{1,0:T(8,128)(2,1)S(1)}, bf16[512,1024]{1,0:T(8,128)(2,1)}, u32[]{:S(2)}) copy-start(bf16[512,1024]{1,0:T(8,128)(2,1)} %param.27) | copy-start | bytes 3145732
  808.5 68.0 %all-gather.27.cloned.1.call-start = ((), (), s32[]{:S(2)}) async-start(), calls=%async_computation.23 | async-start | bytes 3145728 | tf_op jit(solution)/shard_map/all_gather | solution.py:229
  839.6 40.0 %copy-start.63 = (f32[512]{0:T(512)}, f32[512]{0:T(512)S(1)}, u32[]{:S(2)}) copy-start(f32[512]{0:T(512)S(1)} %broadcast_multiply_fusion.2) | copy-start | bytes 6148
  843.2 238.1 %reduce-scatter.37.cloned.1.call-start = ((), (), s32[]{:S(2)}) async-start(), calls=%async_computation.32 | async-start | bytes 540672
  847.5 235.3 %reduce-scatter.21.cloned.1.call-start = ((), (), s32[]{:S(2)}) async-start(), calls=%async_computation.24 | async-start | bytes 3145728 | tf_op jit(solution)/shard_map/reduce_scatter | solution.py:270
  908.3 46.2 %copy-start.42 = (bf16[1024,4,32]{0,2,1:T(8,128)(2,1)S(1)}, bf16[1024,4,32]{0,2,1:T(8,128)(2,1)}, u32[]{:S(2)}) copy-start(bf16[1024,4,32]{0,2,1:T(8,128)(2,1)} %copy-done.41) | copy-start | bytes 786436
  908.3 46.2 %copy-start.44 = (bf16[1024,4,32]{0,2,1:T(8,128)(2,1)S(1)}, bf16[1024,4,32]{0,2,1:T(8,128)(2,1)}, u32[]{:S(2)}) copy-start(bf16[1024,4,32]{0,2,1:T(8,128)(2,1)} %copy-done.43) | copy-start | bytes 786436
  954.5 45.9 %copy-start.25 = (bf16[1024,256]{1,0:T(8,128)(2,1)S(1)}, bf16[1024,256]{1,0:T(8,128)(2,1)}, u32[]{:S(2)}) copy-start(bf16[1024,256]{1,0:T(8,128)(2,1)} %copy-done.24) | copy-start | bytes 1572868
  954.5 46.7 %copy-start.23 = (f32[1024,32]{0,1:T(8,128)S(1)}, f32[1024,32]{0,1:T(8,128)}, u32[]{:S(2)}) copy-start(f32[1024,32]{0,1:T(8,128)} %copy-done.22) | copy-start | bytes 393220
  954.5 46.7 %copy-start.28 = (f32[1024,32]{0,1:T(8,128)S(1)}, f32[1024,32]{0,1:T(8,128)}, u32[]{:S(2)}) copy-start(f32[1024,32]{0,1:T(8,128)} %get-tuple-element.37) | copy-start | bytes 393220
  1007.7 118.0 %reduce-scatter.17.cloned.1.call-start = ((), (), s32[]{:S(2)}) async-start(), calls=%async_computation.20 | async-start | bytes 3145728 | tf_op jit(solution)/shard_map/reduce_scatter | solution.py:173
  1008.3 131.5 %reduce-scatter.27.cloned.1.call-start = ((), (), s32[]{:S(2)}) async-start(), calls=%async_computation.27 | async-start | bytes 1114112 | tf_op jit(solution)/shard_map/reduce_scatter | solution.py:278
  1010.2 190.1 %reduce-scatter.25.cloned.1.call-start = ((), (), s32[]{:S(2)}) async-start(), calls=%async_computation.26 | async-start | bytes 1114112 | tf_op jit(solution)/shard_map/reduce_scatter | solution.py:277
  1012.1 253.4 %reduce-scatter.29.cloned.1.call-start = ((), (), s32[]{:S(2)}) async-start(), calls=%async_computation.28 | async-start | bytes 2228224 | tf_op jit(solution)/shard_map/reduce_scatter | solution.py:279
  1016.8 313.5 %reduce-scatter.23.cloned.1.call-start = ((), (), s32[]{:S(2)}) async-start(), calls=%async_computation.25 | async-start | bytes 2228224 | tf_op jit(solution)/shard_map/reduce_scatter | solution.py:276
  1019.5 493.7 %reduce-scatter.35.cloned.1.call-start = ((), (), s32[]{:S(2)}) async-start(), calls=%async_computation.31 | async-start | bytes 17825792 | tf_op jit(solution)/shard_map/reduce_scatter | solution.py:212
  1043.5 652.4 %reduce-scatter.31.cloned.1.call-start = ((), (), s32[]{:S(2)}) async-start(), calls=%async_computation.29 | async-start | bytes 17825792 | tf_op jit(solution)/shard_map/reduce_scatter | solution.py:210
  1062.4 816.4 %reduce-scatter.33.cloned.1.call-start = ((), (), s32[]{:S(2)}) async-start(), calls=%async_computation.30 | async-start | bytes 17825792 | tf_op jit(solution)/shard_map/reduce_scatter | solution.py:211
  1081.2 44.6 %copy-start.4 = (f32[512,1024]{1,0:T(8,128)S(1)}, f32[512,1024]{1,0:T(8,128)}, u32[]{:S(2)}) copy-start(f32[512,1024]{1,0:T(8,128)} %copy-done.3) | copy-start | bytes 6291460
  1081.2 44.5 %copy-start.51 = (f32[1024]{0:T(1024)S(1)}, f32[1024]{0:T(1024)}, u32[]{:S(2)}) copy-start(f32[1024]{0:T(1024)} %copy-done.49) | copy-start | bytes 12292
  1081.2 44.5 %copy-start.60 = (f32[512]{0:T(512)S(1)}, f32[512]{0:T(512)}, u32[]{:S(2)}) copy-start(f32[512]{0:T(512)} %copy-done.58) | copy-start | bytes 6148
  1081.2 44.5 %copy-start.64 = (f32[512]{0:T(512)S(1)}, f32[512]{0:T(512)}, u32[]{:S(2)}) copy-start(f32[512]{0:T(512)} %copy-done.63) | copy-start | bytes 6148
  (40 other events, 540.9 us)
Sparse Core Ops, SparseCore 0:
  55.7 32.9 all-gather.10
  90.8 37.9 all-gather.12
  131.0 36.8 all-gather.14
  182.6 53.3 reduce-scatter.14
  238.1 34.0 all-gather.24
  274.2 34.2 all-gather.16
  310.9 74.8 all-gather.20
  388.2 73.1 all-gather.18
  463.9 73.1 all-gather.22
  808.6 27.6 reduce-scatter.18
  843.3 33.1 all-gather.26
  878.6 134.1 reduce-scatter.36
  1015.7 27.7 reduce-scatter.20
  1046.1 31.8 reduce-scatter.16
  1082.4 57.3 reduce-scatter.26
  1143.9 56.3 reduce-scatter.24
  1204.9 60.5 reduce-scatter.28
  1269.7 60.6 reduce-scatter.22
  1335.6 177.5 reduce-scatter.34
  1518.3 177.5 reduce-scatter.30
  1701.2 177.5 reduce-scatter.32
where the time goes:
time: 1890 us
  waiting for transfers between devices  884 us (47%)
  matrix products  389 us (21%)
  local copies, waits for them, and re-layouts  316 us (17%)
  blocking collectives  193 us (10%)
  other arithmetic  87.4 us (5%)
    reduce_scatter x1, waiting for transfers between devices, on_device(): lax.psum_scatter(grad_up_w, 'dp', scatter_dimension=1, tiled=True)  183 us
    reduce_scatter x1, waiting for transfers between devices, on_device(): lax.psum_scatter(grad_down_w, 'dp', scatter_dimension=2, tiled=True)  183 us
    reduce_scatter x1, waiting for transfers between devices, on_device(): lax.psum_scatter(grad_gate_w, 'dp', scatter_dimension=1, tiled=True)  183 us
    unnamed x2, blocking collectives  81.7 us
    all_gather x1, blocking collectives, on_device(): lax.all_gather(w_router, ('dp', 'tensor'), axis=0, tiled=True)  68.7 us
    reduce_scatter x1, waiting for transfers between devices, on_device(): lax.psum_scatter(grad_out_w, 'dp', scatter_dimension=1, tiled=True)  65.2 us
    reduce_scatter x1, waiting for transfers between devices, on_device(): lax.psum_scatter(grad_query_w, 'dp', scatter_dimension=0, tiled=True)  64.9 us
    reduce_scatter x1, waiting for transfers between devices, on_device(): lax.psum_scatter(grad_key_w, 'dp', scatter_dimension=0, tiled=True)  60.5 us
  transfers between devices with their start and end apart: 21, of which 11 were waited for; matrix products, arithmetic and copies ran while one was open for 27% of the time, Pallas kernels for 0%

commit v1 on v0

v1 whole, which is shorter than its diff:
```python
import jax
import jax.numpy as jnp
from jax import lax
from jax.experimental import pallas as pl
from jax.experimental.pallas import tpu as pltpu
from jax.sharding import PartitionSpec as P

HEAD = 64
BLOCK = 256


EPSILON = 1e-06
RESIDUAL_SCALE = 0.22
SCORE_SCALE = 0.015625
MASKED = -1e30


def positions(doc_ids):
    index_row = jnp.arange(doc_ids.shape[0], dtype=jnp.int32)
    starting = jnp.concatenate([jnp.ones((1,), dtype=jnp.bool_), doc_ids[1:] != doc_ids[:-1]])
    seg_begin = lax.cummax(jnp.where(starting, index_row, jnp.zeros_like(index_row)), axis=0)
    return index_row - seg_begin


def rotary(places, half_width):
    freqs = 10000.0 ** (-jnp.arange(half_width, dtype=jnp.float32) / half_width)
    angles = freqs[:, None] * places.astype(jnp.float32)[None, :]
    return (jnp.cos(angles), jnp.sin(angles))


def rotate(values, cosine, sine):
    heads = values.reshape(values.shape[0] // HEAD, 2, HEAD // 2, values.shape[1])
    first_half, second_half = heads[:, 0], heads[:, 1]
    return jnp.stack(
        [first_half * cosine - second_half * sine, second_half * cosine + first_half * sine],
        axis=1,
    ).reshape(values.shape)


def norm_back(grad_normed, base, inverse, gain):
    scaled = grad_normed * gain
    return inverse * scaled - base * inverse * jnp.mean(scaled * base, axis=-1, keepdims=True)


def dot(left, right, left_dim=1, right_dim=0):
    return lax.dot_general(
        left, right, (((left_dim,), (right_dim,)), ((), ())), preferred_element_type=jnp.float32
    )


def transposed_dot(left, right):
    return dot(left, right, 1, 1)


def allowed_keys(begin_ref, start, stop):
    shape = (stop, stop - start)
    key = lax.broadcasted_iota(jnp.int32, shape, 0)
    query = lax.broadcasted_iota(jnp.int32, shape, 1) + start
    return (key >= begin_ref[:, start:stop]) & (key <= query)


def attend_kernel(begin_ref, query_ref, key_ref, value_ref, mixed_ref, lse_ref):
    total = key_ref.shape[1]
    keys = (key_ref[...].astype(jnp.float32) * SCORE_SCALE).T.astype(jnp.bfloat16)
    for start in range(0, total, BLOCK):
        stop = start + BLOCK
        allowed = allowed_keys(begin_ref, start, stop)
        for head in range(query_ref.shape[0] // HEAD):
            rows = slice(head * HEAD, (head + 1) * HEAD)
            scores = dot(keys[:stop], query_ref[rows, start:stop])
            scores = jnp.where(allowed, scores, MASKED)
            top = jnp.max(scores, axis=0, keepdims=True)
            expo = jnp.exp(scores - top)
            denom = jnp.sum(expo, axis=0, keepdims=True)
            probs = (expo * (1.0 / denom)).astype(jnp.bfloat16)
            mixed_ref[rows, start:stop] = dot(value_ref[:, :stop], probs).astype(jnp.bfloat16)
            lse_ref[0, head : head + 1, start:stop] = top + jnp.log(denom)


def attend_back_kernel(
    begin_ref,
    query_ref,
    key_ref,
    value_ref,
    lse_ref,
    grad_ref,
    grad_query_ref,
    grad_key_ref,
    grad_value_ref,
):
    total = key_ref.shape[1]
    keys = (key_ref[...].astype(jnp.float32) * SCORE_SCALE).T.astype(jnp.bfloat16)
    values = value_ref[...].astype(jnp.float32).T.astype(jnp.bfloat16)
    grad_key_ref[...] = jnp.zeros_like(grad_key_ref)
    grad_value_ref[...] = jnp.zeros_like(grad_value_ref)
    for start in range(0, total, BLOCK):
        stop = start + BLOCK
        allowed = allowed_keys(begin_ref, start, stop)
        for head in range(query_ref.shape[0] // HEAD):
            rows = slice(head * HEAD, (head + 1) * HEAD)
            query = query_ref[rows, start:stop]
            grad = grad_ref[rows, start:stop]
            scores = dot(keys[:stop], query) - lse_ref[0, head : head + 1, start:stop]
            probs = jnp.exp(jnp.where(allowed, scores, MASKED))
            grad_probs = dot(values[:stop], grad)
            delta = jnp.sum(probs * grad_probs, axis=0, keepdims=True)
            grad_scores = (probs * (grad_probs - delta)).astype(jnp.bfloat16)
            grad_query_ref[rows, start:stop] = SCORE_SCALE * dot(key_ref[:, :stop], grad_scores)
            grad_key_ref[:, :stop] += SCORE_SCALE * transposed_dot(query, grad_scores)
            grad_value_ref[:, :stop] += transposed_dot(grad, probs.astype(jnp.bfloat16))


def attend_call(kernel, begin, query, key, value, extra, outs, work):
    groups = key.shape[0] // HEAD
    total = key.shape[1]

    def spec(array):
        if array.ndim == 3:
            return pl.BlockSpec((1,) + array.shape[1:], lambda g: (g, 0, 0))
        if array.shape[0] == 1:
            return pl.BlockSpec(array.shape, lambda g: (0, 0))
        return pl.BlockSpec((array.shape[0] // groups, total), lambda g: (g, 0))

    operands = (begin, query, key, value) + extra
    return pl.pallas_call(
        kernel,
        out_shape=outs,
        grid=(groups,),
        in_specs=[spec(array) for array in operands],
        out_specs=[spec(array) for array in outs],
        compiler_params=pltpu.CompilerParams(vmem_limit_bytes=40 << 20),
        cost_estimate=pl.CostEstimate(
            flops=work * query.shape[0] * total * total * 2,
            bytes_accessed=sum(array.size * 2 for array in operands),
            transcendentals=query.shape[0] // HEAD * total * total,
        ),
    )(*operands)


def on_device(
    tokens,
    gain_attn,
    gain_ffn,
    w_query,
    w_key,
    w_value,
    w_output,
    w_router,
    w_gate,
    w_up,
    w_down,
    segments,
    routes,
    cotangent,
):
    bf16, f32 = jnp.bfloat16, jnp.float32
    side = lax.axis_index("tensor")
    core = lax.rem(lax.axis_index("dp"), 2)
    dp = lax.axis_size("dp")
    chips = [[2 * chip + one for chip in range(dp // 2)] for one in (0, 1)]
    total = segments.shape[0]
    mine = tokens.shape[0]
    width = tokens.shape[1]
    half = width // 2
    shard = width // dp
    experts, _, hidden_here = w_gate.shape
    heads_here = w_query.shape[1] // HEAD
    groups_here = w_key.shape[1] // HEAD
    query_cols, key_cols = w_query.shape[1], w_key.shape[1]
    qkv_cols = query_cols + 2 * key_cols
    proj_cols = qkv_cols + w_output.shape[0]

    def swap_core(array):
        return lax.ppermute(array, "dp", [(i, i ^ 1) for i in range(dp)])

    def swap_side(array):
        return lax.ppermute(array, "tensor", [(0, 1), (1, 0)])

    def gather(block):
        own = lax.all_gather(block, "dp", axis=0, tiled=True, axis_index_groups=chips)
        return jnp.concatenate([own, swap_core(own)], axis=0)

    def pair_sum(make):
        theirs = swap_core(make(half).astype(bf16))
        return (make(0) + theirs.astype(f32)).astype(bf16)

    def scatter(block):
        return lax.psum_scatter(
            block, "dp", scatter_dimension=0, tiled=True, axis_index_groups=chips
        ).astype(f32)

    def local_columns(array):
        cut = array.reshape(array.shape[0], dp // 2, 2, shard)
        first, second = cut[:, :, 0, :], cut[:, :, 1, :]
        own = jnp.where(core == 0, first, second)
        other = jnp.where(core == 0, second, first)
        return jnp.concatenate(
            [own.reshape(array.shape[0], half), other.reshape(array.shape[0], half)], axis=1
        )

    def global_columns(array):
        own = array[:, :half].reshape(array.shape[0], dp // 2, shard)
        other = array[:, half:].reshape(array.shape[0], dp // 2, shard)
        first = jnp.where(core == 0, own, other)
        second = jnp.where(core == 0, other, own)
        return jnp.stack([first, second], axis=2).reshape(array.shape[0], width)

    def natural_rows(own, other):
        return jnp.where(
            side == 0,
            jnp.concatenate([own, other], axis=0),
            jnp.concatenate([other, own], axis=0),
        )

    def own_rows(array, axis=0):
        return lax.dynamic_slice_in_dim(array, side * mine, mine, axis)

    def other_rows(array, axis=0):
        return lax.dynamic_slice_in_dim(array, (1 - side) * mine, mine, axis)

    def local_rows(array):
        turned = jnp.concatenate([array[mine:], array[:mine]], axis=0)
        return jnp.where(side == 0, array, turned)

    small = jnp.concatenate([gain_attn[:, None], gain_ffn[:, None], w_router], axis=1)
    small_other = swap_side(small)
    small = jnp.where(
        side == 0,
        jnp.concatenate([small, small_other], axis=0),
        jnp.concatenate([small_other, small], axis=0),
    )
    small_cols = small.shape[1]
    small = jnp.pad(small, ((0, 0), (0, 128 - small_cols)))
    packed = gather(jnp.concatenate([w_query, w_key, w_value, w_output.T, small], axis=1))
    gate_w = gather(w_gate.transpose(1, 0, 2).reshape(shard, experts * hidden_here))
    up_w = gather(w_up.transpose(1, 0, 2).reshape(shard, experts * hidden_here))
    down_w = gather(w_down.transpose(2, 0, 1).reshape(shard, experts * hidden_here))
    qkv_w = packed[:, :qkv_cols]
    out_w = packed[:, qkv_cols:proj_cols]
    gain_one = packed[:, proj_cols].astype(f32)
    gain_two = packed[:, proj_cols + 1].astype(f32)
    router = packed[:, proj_cols + 2 : proj_cols + small_cols]

    tokens = local_columns(tokens)
    cotangent = local_columns(cotangent)
    token_rows = natural_rows(tokens, swap_side(tokens)).astype(f32)
    grad_out = cotangent.astype(f32)
    moe_grad = (RESIDUAL_SCALE * grad_out).astype(bf16)
    moe_grad_rows = jnp.concatenate([moe_grad, swap_side(moe_grad)], axis=0)
    places = positions(segments)
    cosine, sine = rotary(places, HEAD // 2)
    begin = (jnp.arange(total, dtype=jnp.int32) - places)[None, :]
    picks = local_rows(routes)
    inverse_one = lax.rsqrt(jnp.mean(token_rows * token_rows, axis=-1, keepdims=True) + EPSILON)
    base_one = token_rows * inverse_one
    rows_one = (base_one * gain_one).astype(bf16)
    qkv = dot(qkv_w, rows_one, 0, 1)
    queries = rotate(qkv[:query_cols], cosine, sine).astype(bf16)
    keys = rotate(qkv[query_cols : query_cols + key_cols], cosine, sine).astype(bf16)
    values = qkv[query_cols + key_cols :].astype(bf16)
    mixed, log_total = attend_call(
        attend_kernel,
        begin,
        queries,
        keys,
        values,
        (),
        [
            jax.ShapeDtypeStruct((query_cols, total), bf16),
            jax.ShapeDtypeStruct((groups_here, heads_here // groups_here, total), f32),
        ],
        2,
    )
    attn_sent = swap_side(dot(other_rows(mixed, 1), out_w, 0, 1).astype(bf16))
    own_tokens = tokens.astype(f32)
    attn_total = dot(own_rows(mixed, 1), out_w, 0, 1) + attn_sent.astype(f32)
    after_attn = own_tokens + RESIDUAL_SCALE * attn_total
    inverse_two = lax.rsqrt(jnp.mean(after_attn * after_attn, axis=-1, keepdims=True) + EPSILON)
    base_two = after_attn * inverse_two
    normed_two = (base_two * gain_two).astype(bf16)
    rows_two = jnp.concatenate([normed_two, swap_side(normed_two)], axis=0)

    logits = dot(rows_two, router)
    expert_ids = jnp.arange(experts, dtype=jnp.int32)
    routed = jnp.any(picks[:, :, None] == expert_ids[None, None, :], axis=1)
    top_logit = jnp.max(jnp.where(routed, logits, MASKED), axis=-1, keepdims=True)
    powers = jnp.where(routed, jnp.exp(jnp.where(routed, logits - top_logit, 0.0)), 0.0)
    gates = powers / jnp.sum(powers, axis=-1, keepdims=True)
    gates_wide = jnp.broadcast_to(gates[:, :, None], (total, experts, hidden_here))
    gates_wide = gates_wide.reshape(total, experts * hidden_here)
    gate_pre = dot(rows_two, gate_w).astype(bf16)
    up_pre = dot(rows_two, up_w).astype(bf16)
    gate_f, up_f = gate_pre.astype(f32), up_pre.astype(f32)
    sigmoid_gate = jax.nn.sigmoid(gate_f)
    activated = gate_f * sigmoid_gate
    hidden = activated * up_f
    hidden_gated = (gates_wide * hidden).astype(bf16)
    moe_sent = swap_side(dot(hidden_gated[mine:], down_w, 1, 1).astype(bf16))
    moe_total = dot(hidden_gated[:mine], down_w, 1, 1) + moe_sent.astype(f32)
    output = after_attn + RESIDUAL_SCALE * moe_total

    grad_plain = dot(moe_grad_rows, down_w).astype(bf16).astype(f32)
    grad_gates = jnp.sum((hidden * grad_plain).reshape(total, experts, hidden_here), axis=-1)
    grad_hidden = gates_wide * grad_plain
    grad_gate_pre = (
        grad_hidden * up_f * sigmoid_gate * (1.0 + gate_f * (1.0 - sigmoid_gate))
    ).astype(bf16)
    grad_up_pre = (grad_hidden * activated).astype(bf16)
    grad_logits = gates * (grad_gates - jnp.sum(gates * grad_gates, axis=-1, keepdims=True))
    logits_high = grad_logits.astype(bf16)
    logits_low = (grad_logits - logits_high.astype(f32)).astype(bf16)
    logits_pair = jnp.concatenate([logits_high, logits_low], axis=1)
    router_pair = jnp.concatenate([router, router], axis=1)

    def rows_two_back(start):
        rows = slice(start, start + mine)
        part = dot(grad_gate_pre[rows], gate_w, 1, 1) + dot(grad_up_pre[rows], up_w, 1, 1)
        return part + dot(logits_pair[rows], router_pair, 1, 1)

    back_sent = swap_side(rows_two_back(mine).astype(bf16))
    grad_normed_two = rows_two_back(0) + back_sent.astype(f32)
    grad_gate_w = pair_sum(lambda at: dot(rows_two[:, at : at + half], grad_gate_pre, 0, 0))
    grad_up_w = pair_sum(lambda at: dot(rows_two[:, at : at + half], grad_up_pre, 0, 0))
    grad_down_w = pair_sum(lambda at: dot(moe_grad_rows[:, at : at + half], hidden_gated, 0, 0))
    grad_router_pair = dot(rows_two, logits_pair, 0, 0)
    grad_router_w = grad_router_pair[:, :experts] + grad_router_pair[:, experts:]

    grad_gain_two = jnp.sum(grad_normed_two * base_two, axis=0)
    grad_after = grad_out + norm_back(grad_normed_two, base_two, inverse_two, gain_two)
    attn_grad = (RESIDUAL_SCALE * grad_after).astype(bf16)
    attn_grad_rows = natural_rows(attn_grad, swap_side(attn_grad))
    attn_grad_rows, grad_gate_w, grad_up_w, grad_down_w = lax.optimization_barrier(
        (attn_grad_rows, grad_gate_w, grad_up_w, grad_down_w)
    )
    grad_gate, grad_up, grad_down = scatter(grad_gate_w), scatter(grad_up_w), scatter(grad_down_w)
    grad_mixed = dot(out_w, attn_grad_rows, 0, 1).astype(bf16)
    grad_query_rot, grad_key_rot, grad_values = attend_call(
        attend_back_kernel,
        begin,
        queries,
        keys,
        values,
        (log_total, grad_mixed),
        [
            jax.ShapeDtypeStruct((query_cols, total), f32),
            jax.ShapeDtypeStruct((key_cols, total), f32),
            jax.ShapeDtypeStruct((key_cols, total), f32),
        ],
        5,
    )
    grad_qkv = jnp.concatenate(
        [
            rotate(grad_query_rot, cosine, -sine).astype(bf16),
            rotate(grad_key_rot, cosine, -sine).astype(bf16),
            grad_values.astype(bf16),
        ],
        axis=0,
    )
    rows_one_sent = dot(other_rows(grad_qkv, 1), qkv_w, 0, 1)
    rows_one_kept = dot(own_rows(grad_qkv, 1), qkv_w, 0, 1)
    sent_back = swap_side(rows_one_sent.astype(bf16))
    grad_gain_one = jnp.sum(rows_one_sent * other_rows(base_one), axis=0)
    grad_gain_one = grad_gain_one + jnp.sum(rows_one_kept * own_rows(base_one), axis=0)
    small_grads = jnp.concatenate(
        [grad_gain_one[:, None], grad_gain_two[:, None], grad_router_w], axis=1
    )
    small_grads = jnp.pad(small_grads, ((0, 0), (0, 128 - small_cols)))

    def packed_part(at):
        cut = slice(at, at + half)
        return jnp.concatenate(
            [
                dot(rows_one[:, cut], grad_qkv, 0, 1),
                dot(attn_grad_rows[:, cut], mixed, 0, 1),
                small_grads[cut],
            ],
            axis=1,
        )

    packed_grads = scatter(pair_sum(packed_part))
    grad_normed_one = rows_one_kept + sent_back.astype(f32)
    grad_tokens = grad_after + norm_back(
        grad_normed_one, own_rows(base_one), own_rows(inverse_one), gain_one
    )
    grad_query = packed_grads[:, :query_cols]
    grad_key = packed_grads[:, query_cols : query_cols + key_cols]
    grad_value = packed_grads[:, query_cols + key_cols : qkv_cols]
    grad_output = packed_grads[:, qkv_cols:proj_cols].T
    small_grads = packed_grads[:, proj_cols : proj_cols + small_cols]
    piece = shard // 2
    upper, lower = small_grads[:piece], small_grads[piece:]
    small_grads = jnp.where(side == 0, upper, lower) + swap_side(jnp.where(side == 0, lower, upper))

    def expert_block(array):
        return array.reshape(shard, experts, hidden_here)

    return (
        global_columns(output),
        global_columns(grad_tokens),
        small_grads[:, 0],
        small_grads[:, 1],
        grad_query,
        grad_key,
        grad_value,
        grad_output,
        small_grads[:, 2:],
        expert_block(grad_gate).transpose(1, 0, 2),
        expert_block(grad_up).transpose(1, 0, 2),
        expert_block(grad_down).transpose(1, 2, 0),
    )


def solution(mesh):
    in_specs = (
        P(("dp", "tensor"), None),
        P(("dp", "tensor")),
        P(("dp", "tensor")),
        P("dp", "tensor"),
        P("dp", "tensor"),
        P("dp", "tensor"),
        P("tensor", "dp"),
        P(("dp", "tensor"), None),
        P(None, "dp", "tensor"),
        P(None, "dp", "tensor"),
        P(None, "tensor", "dp"),
        P("dp"),
        P("dp", None),
        P(("dp", "tensor"), None),
    )
    out_specs = (
        P(("dp", "tensor"), None),
        P(("dp", "tensor"), None),
        P(("dp", "tensor")),
        P(("dp", "tensor")),
        P("dp", "tensor"),
        P("dp", "tensor"),
        P("dp", "tensor"),
        P("tensor", "dp"),
        P(("dp", "tensor"), None),
        P(None, "dp", "tensor"),
        P(None, "dp", "tensor"),
        P(None, "tensor", "dp"),
    )
    return jax.shard_map(
        on_device, mesh=mesh, in_specs=in_specs, out_specs=out_specs, check_vma=False
    )
```

time: 1890 us -> 1000 us (0.53)
  waiting for transfers between devices: 884 us -> 547 us
  local copies, waits for them, and re-layouts: 316 us -> 102 us
  matrix products: 389 us -> 196 us
  blocking collectives: 193 us -> 0 us
  Pallas kernels: 0 us -> 40.2 us
    reduce_scatter x11 -> x4, waiting for transfers between devices: 828 us -> 270 us  [scatter(): lax.psum_scatter(block, 'dp', scatter_dimension=0, tiled=True, axis_index...]
    gather x4 -> x0, local copies, waits for them, and re-layouts: 210 us -> none  [the longest x1 56.8 us: on_device(): grad_in_buffer.reshape(experts * capacity, width)[slot_of]]
    dot_general x30 -> x29, matrix products: 385 us -> 196 us  [dot(): lax.dot_general(left, right, (((left_dim,), (right_dim,)), ((), ())), pre...]
    all_gather x9 -> x4, waiting for transfers between devices: 51.9 us -> 179 us  [gather(): lax.all_gather(block, 'dp', axis=0, tiled=True, axis_index_groups=chips)]
    all_gather x3 -> x0, blocking collectives: 111 us -> none  [the longest x1 68.7 us: on_device(): lax.all_gather(w_router, ('dp', 'tensor'), axis=0, tiled=True)]
    ppermute x0 -> x18, waiting for transfers between devices: none -> 97.3 us  [the longest x10 96 us: swap_side(): return lax.ppermute(array, 'tensor', [(0, 1), (1, 0)])]
    unnamed x2 -> x0, blocking collectives: 81.7 us -> none
    scatter x2 -> x0, local copies, waits for them, and re-layouts: 61.3 us -> none  [the longest x1 30.9 us: on_device(): slot_gate = jnp.zeros((experts * capacity,), jnp.float32).at[slot_of].set...]
  transfers between devices with their start and end apart: 21 -> 26, of which waited for: 11 -> 14; matrix products, arithmetic and copies ran while one was open for 27% -> 21% of each run, Pallas kernels for 0% -> 2%
where the time goes in v1:
time: 1000 us; the launch traced here: 990 us
  waiting for transfers between devices  547 us (55%)
  matrix products  196 us (20%)
  local copies, waits for them, and re-layouts  102 us (10%)
  other arithmetic  72.9 us (7%)
  Pallas kernels  40.2 us (4%)
  starting transfers between devices  15.9 us (2%)
  between operations  15.7 us (2%)
    reduce_scatter x4, waiting for transfers between devices, scatter(): lax.psum_scatter(block, 'dp', scatter_dimension=0, tiled=True, axis_index...  270 us
    dot_general x29, matrix products, dot(): lax.dot_general(left, right, (((left_dim,), (right_dim,)), ((), ())), pre...  196 us
    all_gather x4, waiting for transfers between devices, gather(): lax.all_gather(block, 'dp', axis=0, tiled=True, axis_index_groups=chips)  179 us
    ppermute x10, waiting for transfers between devices, swap_side(): return lax.ppermute(array, 'tensor', [(0, 1), (1, 0)])  96 us
    unnamed x141, local copies, waits for them, and re-layouts  64.3 us
    pallas_call x2, Pallas kernels, attend_call(): pl.pallas_call(kernel, out_shape=outs, grid=(groups,), in_specs=[spec(arr...  40.2 us
    convert_element_type x1, other arithmetic, on_device(): grad_gate_pre = (grad_hidden * up_f * sigmoid_gate * (1.0 + gate_f * (1.0...  22.7 us
  transfers between devices with their start and end apart: 26, of which 14 were waited for; matrix products, arithmetic and copies ran while one was open for 21% of the time, Pallas kernels for 2%

profile of v1, /device:TPU:0, one launch (start us, length us, event | category | flops | bytes accessed | tf_op | source)
XLA Modules:
  0.0 990.3 jit_solution(16304869930604212525)
XLA Ops:
  8.0 3.0 collective-permute-start
  23.9 37.9 %all-gather.5.cloned.1.call-done = bf16[512,1664]{1,0:T(8,128)(2,1)} async-done(((bf16[64,1664]{1,0:T(8,128)(2,1)}), bf16[512,1664]{1,0:T(8,128)(2,1)}) %all-gather.5.cloned.1.call-update) | async-done | bytes 1703952 | tf_op jit(solution)/shard_map/all_gather | solution.py:180
  63.6 8.1 fusion.7
  74.1 10.5 %convert_multiply_fusion.6 = (f32[1024,1024]{1,0:T(8,128)}, bf16[1024,1024]{1,0:T(8,128)(2,1)S(1)}) fusion(f32[1024]{0:T(1024)S(1)} %add_rsqrt_fusion, bf16[512,512]{1,0:T(8,128)(2,1)S(1)} %copy.172, bf16[512,512]{1,0:T(8,128)(2,1)S(1)} %copy.171, bf16[512,1024]{1,0:T(8,128)(2,1)S(1)} %collective-permute-done.2, pred[]{:T(512)S(6)} %eq.11, ...), kind=kLoop, calls=%fused_computation.25 | loop fusion | flops 17825792 | bytes 8396801 | tf_op jit(solution)/shard_map/mul | solution.py:255
  91.5 19.0 %shard_map.229 = (bf16[512,1024]{1,0:T(8,128)(2,1)S(1)}, f32[4,2,1024]{2,1,0:T(2,128)S(1)}) custom-call(s32[1,1024]{1,0:T(1,128)S(1)} %subtract_subtract_fusion.begin_ref, bf16[512,1024]{1,0:T(8,128)(2,1)S(1)} %bitcast.92, bf16[256,1024]{1,0:T(8,128)(2,1)S(1)} %bitcast.94, bf16[256,1024]{1,0:T(8,128)(2,1)S(1)} %slice.442.value_ref), custom_call_target="tpu_custom_call" | custom-call | flops 2147483648 | bytes 2099200 | tf_op jit(solution)/shard_map/pallas_call | solution.py:125
  112.8 24.2 %all-gather.7.cloned.1.call-done = bf16[512,4096]{1,0:T(8,128)(2,1)} async-done(((bf16[64,4096]{1,0:T(8,128)(2,1)}), bf16[512,4096]{1,0:T(8,128)(2,1)}) %all-gather.7.cloned.1.call-update) | async-done | bytes 4194320 | tf_op jit(solution)/shard_map/all_gather | solution.py:180
  137.0 74.4 %all-gather.9.cloned.1.call-done = bf16[512,4096]{1,0:T(8,128)(2,1)} async-done(((bf16[64,4096]{1,0:T(8,128)(2,1)}), bf16[512,4096]{1,0:T(8,128)(2,1)}) %all-gather.9.cloned.1.call-update) | async-done | bytes 4194320 | tf_op jit(solution)/shard_map/all_gather | solution.py:180
  211.4 2.5 multiply_reduce_fusion.5
  221.4 20.3 %collective-permute-done.4 = bf16[512,1024]{1,0:T(8,128)(2,1)} collective-permute-done((bf16[512,1024]{1,0:T(8,128)(2,1)S(1)}, bf16[512,1024]{1,0:T(8,128)(2,1)}, u32[]{:S(2)}, u32[]{:S(2)}) %collective-permute-start.4) | collective-permute-done | bytes 1048608 | tf_op jit(solution)/shard_map/ppermute | solution.py:177
  243.7 41.9 %all-gather.11.cloned.1.call-done = bf16[512,4096]{1,0:T(8,128)(2,1)} async-done(((bf16[64,4096]{1,0:T(8,128)(2,1)}), bf16[512,4096]{1,0:T(8,128)(2,1)}) %all-gather.11.cloned.1.call-update) | async-done | bytes 4194320 | tf_op jit(solution)/shard_map/all_gather | solution.py:180
  285.7 5.0 constant_dynamic-update-slice_fusion.7
  294.9 4.6 constant_dynamic-update-slice_fusion.6
  299.5 4.7 constant_dynamic-update-slice_fusion.8
  304.2 13.6 %convolution_convert_fusion.2 = bf16[1024,4096]{1,0:T(8,128)(2,1)} fusion(bf16[1024,4096]{1,0:T(8,128)(2,1)} %constant_dynamic-update-slice_fusion.6, bf16[512,1024]{1,0:T(8,128)(2,1)} %collective-permute-done.4, bf16[512,1024]{1,0:T(8,128)(2,1)S(1)} %multiply_convert_fusion.4), kind=kOutput, calls=%fused_computation.21 | convolution fusion | flops 8598323200 | bytes 18874368 | tf_op jit(solution)/shard_map/dot_general | solution.py:46
  317.7 13.6 %convolution_convert_fusion.1 = bf16[1024,4096]{1,0:T(8,128)(2,1)} fusion(bf16[1024,4096]{1,0:T(8,128)(2,1)} %constant_dynamic-update-slice_fusion.8, bf16[512,1024]{1,0:T(8,128)(2,1)} %collective-permute-done.4, bf16[512,1024]{1,0:T(8,128)(2,1)S(1)} %multiply_convert_fusion.4), kind=kOutput, calls=%fused_computation.20 | convolution fusion | flops 8598323200 | bytes 18874368 | tf_op jit(solution)/shard_map/dot_general | solution.py:46
  331.9 3.3 copy-done.35
  335.1 22.6 %convert_multiply_fusion.2 = (f32[1024,4096]{1,0:T(8,128)}, bf16[1024,4096]{1,0:T(8,128)(2,1)}) fusion(bf16[1024,4096]{1,0:T(8,128)(2,1)} %convolution_convert_fusion.1, bf16[1024,4096]{1,0:T(8,128)(2,1)} %convolution_convert_fusion.2, bf16[1024,4096]{1,0:T(8,128)(2,1)} %copy-done.35, bf16[512,1024]{1,0:T(8,128)(2,1)} %collective-permute-done.9, ...), kind=kOutput, calls=%fused_computation.3 | convolution fusion | flops 8636071936 | bytes 52428800 | tf_op jit(solution)/shard_map/dot_general | solution.py:46
  357.7 15.7 %copy.210 = f32[128,8,16,256]{3,2,1,0:T(8,128)} copy(f32[128,8,16,256]{3,1,2,0:T(8,128)} %bitcast.99) | data formatting | bytes 33554432
  373.5 8.0 reduce_sum.93
  381.9 2.5 broadcast_in_dim.23
  384.4 19.3 %copy.209 = f32[128,8,16,256]{3,1,2,0:T(8,128)} copy(f32[128,8,16,256]{3,2,1,0:T(8,128)S(1)} %bitcast.97) | data formatting | bytes 33554432
  403.6 22.7 %fusion.2 = (bf16[1024,4096]{1,0:T(8,128)(2,1)}, bf16[1024,4096]{1,0:T(8,128)(2,1)}, bf16[1024,4096]{1,0:T(8,128)(2,1)S(1)}) fusion(bf16[1024,4096]{1,0:T(8,128)(2,1)} %convolution_convert_fusion.1, bf16[1024,4096]{1,0:T(8,128)(2,1)} %convolution_convert_fusion.2, f32[1024,4096]{1,0:T(8,128)} %bitcast.98, bf16[1024,4096]{1,0:T(8,128)(2,1)} %get-tuple-element.152), kind=kLoop, calls=%fused_computation.9 | loop fusion | flops 83886080 | bytes 67108864 | tf_op jit(solution)/shard_map/convert_element_type | solution.py:307
  426.4 13.5 %fusion.12 = f32[512,1024]{1,0:T(8,128)} fusion(bf16[1024,4096]{1,0:T(8,128)(2,1)} %constant_dynamic-update-slice_fusion.8, bf16[1024,4096]{1,0:T(8,128)(2,1)} %get-tuple-element.118), kind=kOutput, calls=%fused_computation.32 | convolution fusion | flops 4294967296 | bytes 14680064 | tf_op jit(solution)/shard_map/dot_general | solution.py:46
  439.9 10.5 %fusion.8 = f32[512,1024]{1,0:T(8,128)} fusion(bf16[1024,4096]{1,0:T(8,128)(2,1)} %constant_dynamic-update-slice_fusion.8, bf16[1024,4096]{1,0:T(8,128)(2,1)} %get-tuple-element.118), kind=kOutput, calls=%fused_computation.28 | convolution fusion | flops 4294967296 | bytes 14680064 | tf_op jit(solution)/shard_map/dot_general | solution.py:46
  450.4 7.4 convolution_convert_fusion.3
  458.2 7.6 convolution_convert_fusion.4
  466.6 10.8 %add_convert_fusion.3 = bf16[512,1024]{1,0:T(8,128)(2,1)} fusion(f32[512,1024]{1,0:T(8,128)S(1)} %fusion.58, f32[512,1024]{1,0:T(8,128)} %fusion.8, bf16[1024,4096]{1,0:T(8,128)(2,1)} %constant_dynamic-update-slice_fusion.6, bf16[1024,4096]{1,0:T(8,128)(2,1)} %get-tuple-element.117), kind=kOutput, calls=%fused_computation.70 | convolution fusion | flops 4296540160 | bytes 17825792 | tf_op jit(solution)/shard_map/dot_general | solution.py:46
  478.9 10.2 %convolution_convert_fusion.5 = bf16[512,4096]{1,0:T(8,128)(2,1)} fusion(bf16[1024,4096]{1,0:T(8,128)(2,1)} %get-tuple-element.117, bf16[512,1024]{1,0:T(8,128)(2,1)S(1)} %copy-done.47, bf16[512,1024]{1,0:T(8,128)(2,1)} %collective-permute-done.4), kind=kOutput, calls=%fused_computation.24 | convolution fusion | flops 4299161600 | bytes 14680064 | tf_op jit(solution)/shard_map/dot_general | solution.py:46
  490.9 12.2 %collective-permute-done.10 = bf16[512,1024]{1,0:T(8,128)(2,1)} collective-permute-done((bf16[512,1024]{1,0:T(8,128)(2,1)}, bf16[512,1024]{1,0:T(8,128)(2,1)}, u32[]{:S(2)}, u32[]{:S(2)}) %collective-permute-start.10) | collective-permute-done | bytes 1048608 | tf_op jit(solution)/shard_map/ppermute | solution.py:177
  503.1 12.8 %multiply_reduce_fusion = (f32[1024]{0:T(1024)S(1)}, f32[512]{0:T(512)S(1)}, f32[512,1024]{1,0:T(8,128)}) fusion(f32[512,1024]{1,0:T(8,128)S(1)} %copy-done.12, f32[512]{0:T(512)S(1)} %copy-done.61, f32[1024]{0:T(1024)S(1)} %copy-done.57, bf16[512,1024]{1,0:T(8,128)(2,1)} %collective-permute-done.10, f32[512,1024]{1,0:T(8,128)} %fusion.59, ...), kind=kOutput, calls=%fused_computation.61 | convolution fusion | flops 4300208640 | bytes 22032384 | tf_op jit(solution)/shard_map/dot_general | solution.py:46
  515.9 3.6 multiply_convert_fusion.3
  521.0 23.1 %collective-permute-done.11 = bf16[512,1024]{1,0:T(8,128)(2,1)S(1)} collective-permute-done((bf16[512,1024]{1,0:T(8,128)(2,1)S(1)}, bf16[512,1024]{1,0:T(8,128)(2,1)S(1)}, u32[]{:S(2)}, u32[]{:S(2)}) %collective-permute-start.11) | collective-permute-done | bytes 1048608 | tf_op jit(solution)/shard_map/ppermute | solution.py:177
  546.5 7.9 add_convert_fusion
  554.4 11.5 %add_convert_fusion.1 = bf16[512,4096]{1,0:T(8,128)(2,1)} fusion(bf16[512,4096]{1,0:T(8,128)(2,1)} %collective-permute-done.13, bf16[1024,4096]{1,0:T(8,128)(2,1)} %get-tuple-element.118, bf16[512,1024]{1,0:T(8,128)(2,1)} %copy-done.46, bf16[512,1024]{1,0:T(8,128)(2,1)} %collective-permute-done.4), kind=kOutput, calls=%fused_computation.17 | convolution fusion | flops 4303355904 | bytes 18874368 | tf_op jit(solution)/shard_map/dot_general | solution.py:46
  565.9 11.5 %add_convert_fusion.2 = bf16[512,4096]{1,0:T(8,128)(2,1)} fusion(bf16[512,4096]{1,0:T(8,128)(2,1)} %collective-permute-done.12, bf16[1024,4096]{1,0:T(8,128)(2,1)} %get-tuple-element.117, bf16[512,1024]{1,0:T(8,128)(2,1)} %copy-done.46, bf16[512,1024]{1,0:T(8,128)(2,1)} %collective-permute-done.4), kind=kOutput, calls=%fused_computation.18 | convolution fusion | flops 4303355904 | bytes 18874368 | tf_op jit(solution)/shard_map/dot_general | solution.py:46
  577.4 3.4 convolution_convert_fusion.7.grad_ref
  580.8 21.3 %shard_map.230 = (f32[512,1024]{1,0:T(8,128)S(1)}, f32[256,1024]{1,0:T(8,128)S(1)}, f32[256,1024]{1,0:T(8,128)S(1)}) custom-call(s32[1,1024]{1,0:T(1,128)S(1)} %copy-done.7, bf16[512,1024]{1,0:T(8,128)(2,1)S(1)} %bitcast.93, bf16[256,1024]{1,0:T(8,128)(2,1)S(1)} %bitcast.95, bf16[256,1024]{1,0:T(8,128)(2,1)S(1)} %copy-done.3, ...), custom_call_target="tpu_custom_call" | custom-call | flops 5368709120 | bytes 3164160 | tf_op jit(solution)/shard_map/pallas_call | solution.py:125
  613.9 16.6 %collective-permute-done.15 = bf16[512,1024]{1,0:T(8,128)(2,1)S(1)} collective-permute-done((bf16[512,1024]{1,0:T(8,128)(2,1)S(1)}, bf16[512,1024]{1,0:T(8,128)(2,1)S(1)}, u32[]{:S(2)}, u32[]{:S(2)}) %collective-permute-start.15) | collective-permute-done | bytes 1048608 | tf_op jit(solution)/shard_map/ppermute | solution.py:177
  630.5 2.8 multiply_reduce_fusion.1
  644.7 9.3 fusion.34
  655.6 23.7 %collective-permute-done.8 = bf16[512,1024]{1,0:T(8,128)(2,1)S(1)} collective-permute-done((bf16[512,1024]{1,0:T(8,128)(2,1)S(1)}, bf16[512,1024]{1,0:T(8,128)(2,1)S(1)}, u32[]{:S(2)}, u32[]{:S(2)}) %collective-permute-start.8) | collective-permute-done | bytes 1048608 | tf_op jit(solution)/shard_map/ppermute | solution.py:177
  679.3 8.3 multiply_add_fusion
  690.3 3.0 copy.198
  693.3 2.8 subtract_add_fusion
  699.3 7.6 reduce-scatter.5.cloned.1.call-done
  714.5 83.1 %reduce-scatter.11.cloned.1.call-done = bf16[64,4096]{1,0:T(8,128)(2,1)} async-done(((bf16[512,4096]{1,0:T(8,128)(2,1)}), bf16[64,4096]{1,0:T(8,128)(2,1)}) %reduce-scatter.11.cloned.1.call-update) | async-done | bytes 524304 | tf_op jit(solution)/shard_map/reduce_scatter | solution.py:188
  799.8 89.3 %reduce-scatter.9.cloned.1.call-done = bf16[64,4096]{1,0:T(8,128)(2,1)} async-done(((bf16[512,4096]{1,0:T(8,128)(2,1)}), bf16[64,4096]{1,0:T(8,128)(2,1)}) %reduce-scatter.9.cloned.1.call-update) | async-done | bytes 524304 | tf_op jit(solution)/shard_map/reduce_scatter | solution.py:188
  891.3 89.5 %reduce-scatter.7.cloned.1.call-done = bf16[64,4096]{1,0:T(8,128)(2,1)} async-done(((bf16[512,4096]{1,0:T(8,128)(2,1)}), bf16[64,4096]{1,0:T(8,128)(2,1)}) %reduce-scatter.7.cloned.1.call-update) | async-done | bytes 524304 | tf_op jit(solution)/shard_map/reduce_scatter | solution.py:188
  (286 shorter events, 93.7 us)
Async XLA Ops:
  7.2 54.6 %all-gather.5.cloned.1.call-start = ((), (), s32[]{:S(2)}) async-start(), calls=%async_computation.4 | async-start | bytes 1916928 | tf_op jit(solution)/shard_map/all_gather | solution.py:180
  8.0 6.2 collective-permute-start
  16.1 120.9 %all-gather.7.cloned.1.call-start = ((), (), s32[]{:S(2)}) async-start(), calls=%async_computation.5 | async-start | bytes 4718592 | tf_op jit(solution)/shard_map/all_gather | solution.py:180
  18.0 193.4 %all-gather.9.cloned.1.call-start = ((), (), s32[]{:S(2)}) async-start(), calls=%async_computation.6 | async-start | bytes 4718592 | tf_op jit(solution)/shard_map/all_gather | solution.py:180
  20.0 265.7 %all-gather.11.cloned.1.call-start = ((), (), s32[]{:S(2)}) async-start(), calls=%async_computation.7 | async-start | bytes 4718592 | tf_op jit(solution)/shard_map/all_gather | solution.py:180
  21.3 42.4 %collective-permute-start.2 = (bf16[512,1024]{1,0:T(8,128)(2,1)S(1)}, bf16[512,1024]{1,0:T(8,128)(2,1)S(1)}, u32[]{:S(2)}, u32[]{:S(2)}) collective-permute-start(bf16[512,1024]{1,0:T(8,128)(2,1)S(1)} %pad_maximum_fusion.7), channel_id=1, source_target_pairs={{0,1},{1,0},{2,3},{3,2},{4,5},{5,4},{6,7},{7,6},{8,9},{9,8},{10,11... | collective-permute-start | bytes 3145736 | tf_op jit(solution)/shard_map/ppermute | solution.py:177
  23.6 683.3 %reduce-scatter.5.cloned.1.call-start = ((), (), s32[]{:S(2)}) async-start(), calls=%async_computation.8 | async-start | bytes 1916928 | tf_op jit(solution)/shard_map/reduce_scatter | solution.py:188
  61.8 10.1 %collective-permute-start.1 = (bf16[512,1664]{1,0:T(8,128)(2,1)}, bf16[512,1664]{1,0:T(8,128)(2,1)}, u32[]{:S(2)}, u32[]{:S(2)}) collective-permute-start(bf16[512,1664]{1,0:T(8,128)(2,1)} %all-gather.5.cloned.1.call-done), channel_id=1, source_target_pairs={{0,2},{2,0},{4,6},{6,4},{8,10},{10,8},{12,14},{14,12},{16,18},{18,... | collective-permute-start | bytes 5111816 | tf_op jit(solution)/shard_map/ppermute | solution.py:174
  62.4 29.1 %copy-start.6 = (s32[1,1024]{1,0:T(1,128)}, s32[1,1024]{1,0:T(1,128)S(1)}, u32[]{:S(2)}) copy-start(s32[1,1024]{1,0:T(1,128)S(1)} %subtract_subtract_fusion.begin_ref) | copy-start | bytes 12292
  63.6 25.6 %copy-start.30 = (f32[32,1024]{1,0:T(8,128)}, f32[32,1024]{1,0:T(8,128)S(1)}, u32[]{:S(2)}) copy-start(f32[32,1024]{1,0:T(8,128)S(1)} %get-tuple-element.148) | copy-start | bytes 393220
  73.8 36.7 %copy-start.17 = (bf16[1024,1664]{1,0:T(8,128)(2,1)}, bf16[1024,1664]{1,0:T(8,128)(2,1)S(1)}, u32[]{:S(2)}) copy-start(bf16[1024,1664]{1,0:T(8,128)(2,1)S(1)} %constant_dynamic-update-slice_fusion.4) | copy-start | bytes 10223620
  74.1 139.9 %copy-start.56 = (f32[1024]{0:T(1024)}, f32[1024]{0:T(1024)S(1)}, u32[]{:S(2)}) copy-start(f32[1024]{0:T(1024)S(1)} %get-tuple-element.107) | copy-start | bytes 12292
  89.2 21.2 %copy-start.4 = (bf16[4,2,32,1024]{3,2,1,0:T(8,128)(2,1)}, bf16[4,2,32,1024]{3,2,1,0:T(8,128)(2,1)S(1)}, u32[]{:S(2)}) copy-start(bf16[4,2,32,1024]{3,2,1,0:T(8,128)(2,1)S(1)} %pad_maximum_fusion.11) | copy-start | bytes 1572868
  91.5 19.0 %copy-start = (bf16[8,2,32,1024]{3,2,1,0:T(8,128)(2,1)}, bf16[8,2,32,1024]{3,2,1,0:T(8,128)(2,1)S(1)}, u32[]{:S(2)}) copy-start(bf16[8,2,32,1024]{3,2,1,0:T(8,128)(2,1)S(1)} %pad_maximum_fusion.8) | copy-start | bytes 3145732
  110.5 103.5 %copy-start.8 = (bf16[512,1024]{1,0:T(8,128)(2,1)}, bf16[512,1024]{1,0:T(8,128)(2,1)S(1)}, u32[]{:S(2)}) copy-start(bf16[512,1024]{1,0:T(8,128)(2,1)S(1)} %get-tuple-element.21) | copy-start | bytes 3145732
  111.3 100.1 %collective-permute-start.3 = (bf16[512,1024]{1,0:T(8,128)(2,1)S(1)}, bf16[512,1024]{1,0:T(8,128)(2,1)}, u32[]{:S(2)}, u32[]{:S(2)}) collective-permute-start(bf16[512,1024]{1,0:T(8,128)(2,1)S(1)} %convolution_convert_fusion.8), channel_id=1, source_target_pairs={{0,1},{1,0},{2,3},{3,2},{4,5},{5,4},{6,7},{7,6},{8,9},{9,8},{10,11... | collective-permute-start | bytes 3145736 | tf_op jit(solution)/shard_map/ppermute | solution.py:177
  137.0 157.9 %collective-permute-start.5 = (bf16[512,4096]{1,0:T(8,128)(2,1)}, bf16[512,4096]{1,0:T(8,128)(2,1)}, u32[]{:S(2)}, u32[]{:S(2)}) collective-permute-start(bf16[512,4096]{1,0:T(8,128)(2,1)} %all-gather.7.cloned.1.call-done), channel_id=1, source_target_pairs={{0,2},{2,0},{4,6},{6,4},{8,10},{10,8},{12,14},{14,12},{16,18},{18,... | collective-permute-start | bytes 12582920 | tf_op jit(solution)/shard_map/ppermute | solution.py:174
  211.4 88.1 %collective-permute-start.6 = (bf16[512,4096]{1,0:T(8,128)(2,1)}, bf16[512,4096]{1,0:T(8,128)(2,1)}, u32[]{:S(2)}, u32[]{:S(2)}) collective-permute-start(bf16[512,4096]{1,0:T(8,128)(2,1)} %all-gather.9.cloned.1.call-done), channel_id=1, source_target_pairs={{0,2},{2,0},{4,6},{6,4},{8,10},{10,8},{12,14},{14,12},{16,18},{18,... | collective-permute-start | bytes 12582920 | tf_op jit(solution)/shard_map/ppermute | solution.py:174
  215.5 242.7 %copy-start.46 = (bf16[512,1024]{1,0:T(8,128)(2,1)}, bf16[512,1024]{1,0:T(8,128)(2,1)S(1)}, u32[]{:S(2)}) copy-start(bf16[512,1024]{1,0:T(8,128)(2,1)S(1)} %multiply_convert_fusion.4) | copy-start | bytes 3145732
  215.5 26.1 %collective-permute-start.4 = (bf16[512,1024]{1,0:T(8,128)(2,1)S(1)}, bf16[512,1024]{1,0:T(8,128)(2,1)}, u32[]{:S(2)}, u32[]{:S(2)}) collective-permute-start(bf16[512,1024]{1,0:T(8,128)(2,1)S(1)} %multiply_convert_fusion.4), channel_id=1, source_target_pairs={{0,1},{1,0},{2,3},{3,2},{4,5},{5,4},{6,7},{7,6},{8,9},{9,8},{10,11... | collective-permute-start | bytes 3145736 | tf_op jit(solution)/shard_map/ppermute | solution.py:177
  218.3 25.3 %copy-start.20 = (bf16[512,512]{1,0:T(8,128)(2,1)}, bf16[512,512]{1,0:T(8,128)(2,1)S(1)}, u32[]{:S(2)}) copy-start(bf16[512,512]{1,0:T(8,128)(2,1)S(1)} %copy.183) | copy-start | bytes 1572868
  218.6 72.1 %copy-start.22 = (bf16[512,512]{1,0:T(8,128)(2,1)}, bf16[512,512]{1,0:T(8,128)(2,1)S(1)}, u32[]{:S(2)}) copy-start(bf16[512,512]{1,0:T(8,128)(2,1)S(1)} %copy.184) | copy-start | bytes 1572868
  218.8 231.6 %copy-start.49 = (bf16[512,1024]{1,0:T(8,128)(2,1)}, bf16[512,1024]{1,0:T(8,128)(2,1)S(1)}, u32[]{:S(2)}) copy-start(bf16[512,1024]{1,0:T(8,128)(2,1)S(1)} %fusion.21) | copy-start | bytes 3145732
  218.8 116.3 %collective-permute-start.9 = (bf16[512,1024]{1,0:T(8,128)(2,1)S(1)}, bf16[512,1024]{1,0:T(8,128)(2,1)}, u32[]{:S(2)}, u32[]{:S(2)}) collective-permute-start(bf16[512,1024]{1,0:T(8,128)(2,1)S(1)} %fusion.21), channel_id=1, source_target_pairs={{0,1},{1,0},{2,3},{3,2},{4,5},{5,4},{6,7},{7,6},{8,9},{9,8},{10,11... | collective-permute-start | bytes 3145736 | tf_op jit(solution)/shard_map/ppermute | solution.py:177
  285.7 45.7 %collective-permute-start.7 = (bf16[512,4096]{1,0:T(8,128)(2,1)}, bf16[512,4096]{1,0:T(8,128)(2,1)S(1)}, u32[]{:S(2)}, u32[]{:S(2)}) collective-permute-start(bf16[512,4096]{1,0:T(8,128)(2,1)} %all-gather.11.cloned.1.call-done), channel_id=1, source_target_pairs={{0,2},{2,0},{4,6},{6,4},{8,10},{10,8},{12,14},{14,12},{16,18},{18,... | collective-permute-start | bytes 12582920 | tf_op jit(solution)/shard_map/ppermute | solution.py:174
  426.4 120.1 %copy-start.15 = (bf16[1024,4096]{1,0:T(8,128)(2,1)}, bf16[1024,4096]{1,0:T(8,128)(2,1)S(1)}, u32[]{:S(2)}) copy-start(bf16[1024,4096]{1,0:T(8,128)(2,1)S(1)} %get-tuple-element.119) | copy-start | bytes 25165828
  457.8 88.6 %collective-permute-start.14 = (bf16[512,4096]{1,0:T(8,128)(2,1)}, bf16[512,4096]{1,0:T(8,128)(2,1)}, u32[]{:S(2)}, u32[]{:S(2)}) collective-permute-start(bf16[512,4096]{1,0:T(8,128)(2,1)} %convolution_convert_fusion.3), channel_id=1, source_target_pairs={{0,2},{2,0},{4,6},{6,4},{8,10},{10,8},{12,14},{14,12},{16,18},{18,... | collective-permute-start | bytes 12582920 | tf_op jit(solution)/shard_map/ppermute | solution.py:174
  465.8 88.6 %collective-permute-start.13 = (bf16[512,4096]{1,0:T(8,128)(2,1)}, bf16[512,4096]{1,0:T(8,128)(2,1)}, u32[]{:S(2)}, u32[]{:S(2)}) collective-permute-start(bf16[512,4096]{1,0:T(8,128)(2,1)} %convolution_convert_fusion.4), channel_id=1, source_target_pairs={{0,2},{2,0},{4,6},{6,4},{8,10},{10,8},{12,14},{14,12},{16,18},{18,... | collective-permute-start | bytes 12582920 | tf_op jit(solution)/shard_map/ppermute | solution.py:174
  477.4 25.8 %copy-start.12 = (f32[512,1024]{1,0:T(8,128)S(1)}, f32[512,1024]{1,0:T(8,128)}, u32[]{:S(2)}) copy-start(f32[512,1024]{1,0:T(8,128)} %copy-done.11) | copy-start | bytes 6291460
  477.4 25.8 %copy-start.57 = (f32[1024]{0:T(1024)S(1)}, f32[1024]{0:T(1024)}, u32[]{:S(2)}) copy-start(f32[1024]{0:T(1024)} %copy-done.56) | copy-start | bytes 12292
  477.4 25.8 %copy-start.61 = (f32[512]{0:T(512)S(1)}, f32[512]{0:T(512)}, u32[]{:S(2)}) copy-start(f32[512]{0:T(512)} %copy-done.60) | copy-start | bytes 6148
  477.4 25.7 %collective-permute-start.10 = (bf16[512,1024]{1,0:T(8,128)(2,1)}, bf16[512,1024]{1,0:T(8,128)(2,1)}, u32[]{:S(2)}, u32[]{:S(2)}) collective-permute-start(bf16[512,1024]{1,0:T(8,128)(2,1)} %add_convert_fusion.3), channel_id=1, source_target_pairs={{0,1},{1,0},{2,3},{3,2},{4,5},{5,4},{6,7},{7,6},{8,9},{9,8},{10,11... | collective-permute-start | bytes 3145736 | tf_op jit(solution)/shard_map/ppermute | solution.py:177
  489.1 76.8 %collective-permute-start.12 = (bf16[512,4096]{1,0:T(8,128)(2,1)}, bf16[512,4096]{1,0:T(8,128)(2,1)}, u32[]{:S(2)}, u32[]{:S(2)}) collective-permute-start(bf16[512,4096]{1,0:T(8,128)(2,1)} %convolution_convert_fusion.5), channel_id=1, source_target_pairs={{0,2},{2,0},{4,6},{6,4},{8,10},{10,8},{12,14},{14,12},{16,18},{18,... | collective-permute-start | bytes 12582920 | tf_op jit(solution)/shard_map/ppermute | solution.py:174
  490.9 25.0 %copy-start.21 = (bf16[512,512]{1,0:T(8,128)(2,1)S(1)}, bf16[512,512]{1,0:T(8,128)(2,1)}, u32[]{:S(2)}) copy-start(bf16[512,512]{1,0:T(8,128)(2,1)} %copy-done.20) | copy-start | bytes 1572868
  490.9 25.0 %copy-start.23 = (bf16[512,512]{1,0:T(8,128)(2,1)S(1)}, bf16[512,512]{1,0:T(8,128)(2,1)}, u32[]{:S(2)}) copy-start(bf16[512,512]{1,0:T(8,128)(2,1)} %copy-done.22) | copy-start | bytes 1572868
  519.5 26.9 %copy-start.50 = (bf16[512,1024]{1,0:T(8,128)(2,1)S(1)}, bf16[512,1024]{1,0:T(8,128)(2,1)}, u32[]{:S(2)}) copy-start(bf16[512,1024]{1,0:T(8,128)(2,1)} %copy-done.49) | copy-start | bytes 3145732
  519.5 24.6 %collective-permute-start.11 = (bf16[512,1024]{1,0:T(8,128)(2,1)S(1)}, bf16[512,1024]{1,0:T(8,128)(2,1)S(1)}, u32[]{:S(2)}, u32[]{:S(2)}) collective-permute-start(bf16[512,1024]{1,0:T(8,128)(2,1)S(1)} %get-tuple-element.111), channel_id=1, source_target_pairs={{0,1},{1,0},{2,3},{3,2},{4,5},{5,4},{6,7},{7,6},{8,9},{9,8},{10,11... | collective-permute-start | bytes 3145736 | tf_op jit(solution)/shard_map/ppermute | solution.py:177
  580.8 21.3 %copy-start.31 = (f32[32,1024]{1,0:T(8,128)S(1)}, f32[32,1024]{1,0:T(8,128)}, u32[]{:S(2)}) copy-start(f32[32,1024]{1,0:T(8,128)} %copy-done.30) | copy-start | bytes 393220
  580.8 21.3 %copy-start.43 = (f32[32,1024]{1,0:T(8,128)S(1)}, f32[32,1024]{1,0:T(8,128)}, u32[]{:S(2)}) copy-start(f32[32,1024]{1,0:T(8,128)} %get-tuple-element.146) | copy-start | bytes 393220
  606.7 23.8 %collective-permute-start.15 = (bf16[512,1024]{1,0:T(8,128)(2,1)S(1)}, bf16[512,1024]{1,0:T(8,128)(2,1)S(1)}, u32[]{:S(2)}, u32[]{:S(2)}) collective-permute-start(bf16[512,1024]{1,0:T(8,128)(2,1)S(1)} %get-tuple-element.156), channel_id=1, source_target_pairs={{0,1},{1,0},{2,3},{3,2},{4,5},{5,4},{6,7},{7,6},{8,9},{9,8},{10,11... | collective-permute-start | bytes 3145736 | tf_op jit(solution)/shard_map/ppermute | solution.py:177
  611.6 18.9 %copy-start.10 = (f32[1024,1024]{1,0:T(8,128)S(1)}, f32[1024,1024]{1,0:T(8,128)}, u32[]{:S(2)}) copy-start(f32[1024,1024]{1,0:T(8,128)} %get-tuple-element.124) | copy-start | bytes 12582916
  611.6 18.9 %copy-start.55 = (f32[1024]{0:T(1024)S(1)}, f32[1024]{0:T(1024)}, u32[]{:S(2)}) copy-start(f32[1024]{0:T(1024)} %copy-done.54) | copy-start | bytes 12292
  637.2 3.7 collective-permute-start.16
  642.6 155.0 %reduce-scatter.11.cloned.1.call-start = ((), (), s32[]{:S(2)}) async-start(), calls=%async_computation.11 | async-start | bytes 4718592 | tf_op jit(solution)/shard_map/reduce_scatter | solution.py:188
  643.2 245.9 %reduce-scatter.9.cloned.1.call-start = ((), (), s32[]{:S(2)}) async-start(), calls=%async_computation.10 | async-start | bytes 4718592 | tf_op jit(solution)/shard_map/reduce_scatter | solution.py:188
  643.9 336.9 %reduce-scatter.7.cloned.1.call-start = ((), (), s32[]{:S(2)}) async-start(), calls=%async_computation.9 | async-start | bytes 4718592 | tf_op jit(solution)/shard_map/reduce_scatter | solution.py:188
  654.0 25.2 %collective-permute-start.8 = (bf16[512,1024]{1,0:T(8,128)(2,1)S(1)}, bf16[512,1024]{1,0:T(8,128)(2,1)S(1)}, u32[]{:S(2)}, u32[]{:S(2)}) collective-permute-start(bf16[512,1024]{1,0:T(8,128)(2,1)S(1)} %fusion.34), channel_id=1, source_target_pairs={{0,1},{1,0},{2,3},{3,2},{4,5},{5,4},{6,7},{7,6},{8,9},{9,8},{10,11... | collective-permute-start | bytes 3145736 | tf_op jit(solution)/shard_map/ppermute | solution.py:177
  707.9 5.2 collective-permute-start.17
  (42 other events, 190.1 us)
Sparse Core Ops, SparseCore 0:
  16.2 45.5 all-gather.4
  64.5 72.4 all-gather.6
  139.7 71.6 all-gather.8
  214.0 71.6 all-gather.10
  642.7 64.1 reduce-scatter.4
  710.9 86.7 reduce-scatter.10
  801.3 87.7 reduce-scatter.8
  893.2 87.6 reduce-scatter.6

commit v2 on v1

--- a/solution.py
+++ b/solution.py
@@ -137,6 +137,75 @@
     )(*operands)
 
 
+def pick_column(gates_ref):
+    expert = lax.broadcasted_iota(jnp.int32, gates_ref.shape, 1) == pl.program_id(0)
+    return expert, jnp.sum(jnp.where(expert, gates_ref[...], 0.0), axis=1, keepdims=True)
+
+
+def expert_kernel(rows_ref, gate_w_ref, up_w_ref, gates_ref, gate_ref, up_ref, hidden_ref):
+    _, gate_column = pick_column(gates_ref)
+    for start in range(0, rows_ref.shape[0], BLOCK):
+        cut = slice(start, start + BLOCK)
+        gate = dot(rows_ref[cut, :], gate_w_ref[...])
+        up = dot(rows_ref[cut, :], up_w_ref[...])
+        gate_ref[cut, :] = gate.astype(jnp.bfloat16)
+        up_ref[cut, :] = up.astype(jnp.bfloat16)
+        hidden = gate * jax.nn.sigmoid(gate) * up
+        hidden_ref[cut, :] = (gate_column[cut] * hidden).astype(jnp.bfloat16)
+
+
+def expert_back_kernel(
+    grad_rows_ref,
+    down_w_ref,
+    gate_ref,
+    up_ref,
+    gates_ref,
+    grad_gate_ref,
+    grad_up_ref,
+    grad_gates_ref,
+):
+    expert, gate_column = pick_column(gates_ref)
+
+    @pl.when(pl.program_id(0) == 0)
+    def _():
+        grad_gates_ref[...] = jnp.zeros_like(grad_gates_ref)
+
+    for start in range(0, grad_rows_ref.shape[0], BLOCK):
+        cut = slice(start, start + BLOCK)
+        plain = dot(grad_rows_ref[cut, :], down_w_ref[...])
+        gate = gate_ref[cut, :].astype(jnp.float32)
+        up = up_ref[cut, :].astype(jnp.float32)
+        sigmoid_gate = jax.nn.sigmoid(gate)
+        activated = gate * sigmoid_gate
+        grad_column = jnp.sum(activated * up * plain, axis=1, keepdims=True)
+        grad_gates_ref[cut, :] += jnp.where(expert[cut], grad_column, 0.0)
+        grad_hidden = gate_column[cut] * plain
+        slope = sigmoid_gate * (1.0 + gate * (1.0 - sigmoid_gate))
+        grad_gate_ref[cut, :] = (grad_hidden * up * slope).astype(jnp.bfloat16)
+        grad_up_ref[cut, :] = (grad_hidden * activated).astype(jnp.bfloat16)
+
+
+def expert_call(kernel, operands, outs, experts, work):
+    def spec(array):
+        if array.shape[1] < experts * BLOCK:
+            return pl.BlockSpec(array.shape, lambda e: (0, 0))
+        return pl.BlockSpec((array.shape[0], array.shape[1] // experts), lambda e: (0, e))
+
+    return pl.pallas_call(
+        kernel,
+        out_shape=outs,
+        grid=(experts,),
+        in_specs=[spec(array) for array in operands],
+        out_specs=[spec(array) for array in outs],
+        compiler_params=pltpu.CompilerParams(vmem_limit_bytes=40 << 20),
+        cost_estimate=pl.CostEstimate(
+            flops=2 * work,
+            bytes_accessed=sum(array.size * 2 for array in operands),
+            transcendentals=outs[0].size,
+        ),
+    )(*operands)
+
+
 def on_device(
     tokens,
     gain_attn,
@@ -156,12 +225,15 @@
     bf16, f32 = jnp.bfloat16, jnp.float32
     side = lax.axis_index("tensor")
     core = lax.rem(lax.axis_index("dp"), 2)
+    near = lax.rem(lax.axis_index("dp") // 2, 2)
     dp = lax.axis_size("dp")
-    chips = [[2 * chip + one for chip in range(dp // 2)] for one in (0, 1)]
+    far = dp // 4
+    lines = [[4 * step + first for step in range(far)] for first in range(4)]
     total = segments.shape[0]
     mine = tokens.shape[0]
     width = tokens.shape[1]
     half = width // 2
+    quarter = width // 4
     shard = width // dp
     experts, _, hidden_here = w_gate.shape
     heads_here = w_query.shape[1] // HEAD
@@ -176,34 +248,44 @@
     def swap_side(array):
         return lax.ppermute(array, "tensor", [(0, 1), (1, 0)])
 
+    def swap_near(array):
+        return lax.ppermute(array, "dp", [(i, i ^ 2) for i in range(dp)])
+
     def gather(block):
-        own = lax.all_gather(block, "dp", axis=0, tiled=True, axis_index_groups=chips)
+        own = lax.all_gather(block, "dp", axis=0, tiled=True, axis_index_groups=lines)
+        own = jnp.concatenate([own, swap_near(own)], axis=0)
         return jnp.concatenate([own, swap_core(own)], axis=0)
 
     def pair_sum(make):
         theirs = swap_core(make(half).astype(bf16))
         return (make(0) + theirs.astype(f32)).astype(bf16)
 
+    def near_sum(block):
+        theirs = swap_near(block[quarter:])
+        return (block[:quarter].astype(f32) + theirs.astype(f32)).astype(bf16)
+
     def scatter(block):
         return lax.psum_scatter(
-            block, "dp", scatter_dimension=0, tiled=True, axis_index_groups=chips
+            block, "dp", scatter_dimension=0, tiled=True, axis_index_groups=lines
         ).astype(f32)
 
+    def own_first(flag, array, axis):
+        first = lax.index_in_dim(array, 0, axis, keepdims=False)
+        second = lax.index_in_dim(array, 1, axis, keepdims=False)
+        return jnp.where(flag == 0, first, second), jnp.where(flag == 0, second, first)
+
     def local_columns(array):
-        cut = array.reshape(array.shape[0], dp // 2, 2, shard)
-        first, second = cut[:, :, 0, :], cut[:, :, 1, :]
-        own = jnp.where(core == 0, first, second)
-        other = jnp.where(core == 0, second, first)
-        return jnp.concatenate(
-            [own.reshape(array.shape[0], half), other.reshape(array.shape[0], half)], axis=1
-        )
+        cut = array.reshape(array.shape[0], far, 2, 2, shard)
+        pieces = []
+        for side_piece in own_first(core, cut, 3):
+            pieces.extend(own_first(near, side_piece, 2))
+        return jnp.concatenate([one.reshape(array.shape[0], quarter) for one in pieces], axis=1)
 
     def global_columns(array):
-        own = array[:, :half].reshape(array.shape[0], dp // 2, shard)
-        other = array[:, half:].reshape(array.shape[0], dp // 2, shard)
-        first = jnp.where(core == 0, own, other)
-        second = jnp.where(core == 0, other, own)
-        return jnp.stack([first, second], axis=2).reshape(array.shape[0], width)
+        cut = array.reshape(array.shape[0], 2, 2, far, shard)
+        halves = own_first(core, cut, 1)
+        halves = [jnp.stack(own_first(near, one, 1), axis=2) for one in halves]
+        return jnp.stack(halves, axis=3).reshape(array.shape[0], width)
 
     def natural_rows(own, other):
         return jnp.where(
@@ -286,26 +368,22 @@
     top_logit = jnp.max(jnp.where(routed, logits, MASKED), axis=-1, keepdims=True)
     powers = jnp.where(routed, jnp.exp(jnp.where(routed, logits - top_logit, 0.0)), 0.0)
     gates = powers / jnp.sum(powers, axis=-1, keepdims=True)
-    gates_wide = jnp.broadcast_to(gates[:, :, None], (total, experts, hidden_here))
-    gates_wide = gates_wide.reshape(total, experts * hidden_here)
-    gate_pre = dot(rows_two, gate_w).astype(bf16)
-    up_pre = dot(rows_two, up_w).astype(bf16)
-    gate_f, up_f = gate_pre.astype(f32), up_pre.astype(f32)
-    sigmoid_gate = jax.nn.sigmoid(gate_f)
-    activated = gate_f * sigmoid_gate
-    hidden = activated * up_f
-    hidden_gated = (gates_wide * hidden).astype(bf16)
+    wide = jax.ShapeDtypeStruct((total, experts * hidden_here), bf16)
+    matmul = total * width * experts * hidden_here
+    gate_pre, up_pre, hidden_gated = expert_call(
+        expert_kernel, (rows_two, gate_w, up_w, gates), [wide] * 3, experts, 2 * matmul
+    )
     moe_sent = swap_side(dot(hidden_gated[mine:], down_w, 1, 1).astype(bf16))
     moe_total = dot(hidden_gated[:mine], down_w, 1, 1) + moe_sent.astype(f32)
     output = after_attn + RESIDUAL_SCALE * moe_total
 
-    grad_plain = dot(moe_grad_rows, down_w).astype(bf16).astype(f32)
-    grad_gates = jnp.sum((hidden * grad_plain).reshape(total, experts, hidden_here), axis=-1)
-    grad_hidden = gates_wide * grad_plain
-    grad_gate_pre = (
-        grad_hidden * up_f * sigmoid_gate * (1.0 + gate_f * (1.0 - sigmoid_gate))
-    ).astype(bf16)
-    grad_up_pre = (grad_hidden * activated).astype(bf16)
+    grad_gate_pre, grad_up_pre, grad_gates = expert_call(
+        expert_back_kernel,
+        (moe_grad_rows, down_w, gate_pre, up_pre, gates),
+        [wide, wide, jax.ShapeDtypeStruct((total, experts), f32)],
+        experts,
+        matmul,
+    )
     grad_logits = gates * (grad_gates - jnp.sum(gates * grad_gates, axis=-1, keepdims=True))
     logits_high = grad_logits.astype(bf16)
     logits_low = (grad_logits - logits_high.astype(f32)).astype(bf16)
@@ -332,7 +410,9 @@
     attn_grad_rows, grad_gate_w, grad_up_w, grad_down_w = lax.optimization_barrier(
         (attn_grad_rows, grad_gate_w, grad_up_w, grad_down_w)
     )
-    grad_gate, grad_up, grad_down = scatter(grad_gate_w), scatter(grad_up_w), scatter(grad_down_w)
+    grad_gate = scatter(near_sum(grad_gate_w))
+    grad_up = scatter(near_sum(grad_up_w))
+    grad_down = scatter(near_sum(grad_down_w))
     grad_mixed = dot(out_w, attn_grad_rows, 0, 1).astype(bf16)
     grad_query_rot, grad_key_rot, grad_values = attend_call(
         attend_back_kernel,
@@ -377,7 +457,11 @@
             axis=1,
         )
 
-    packed_grads = scatter(pair_sum(packed_part))
+    packed_grads = near_sum(pair_sum(packed_part))
+    packed_grads, grad_gate, grad_up, grad_down = lax.optimization_barrier(
+        (packed_grads, grad_gate, grad_up, grad_down)
+    )
+    packed_grads = scatter(packed_grads)
     grad_normed_one = rows_one_kept + sent_back.astype(f32)
     grad_tokens = grad_after + norm_back(
         grad_normed_one, own_rows(base_one), own_rows(inverse_one), gain_one

time: 1000 us -> 724 us (0.72)
  waiting for transfers between devices: 547 us -> 250 us
  matrix products: 196 us -> 134 us
  Pallas kernels: 40.2 us -> 93.1 us
  blocking collectives: 0 us -> 32.3 us
  local copies, waits for them, and re-layouts: 102 us -> 88.2 us
    reduce_scatter x4, waiting for transfers between devices: 270 us -> 12 us  [scatter(): lax.psum_scatter(block, 'dp', scatter_dimension=0, tiled=True, axis_index...]
    ppermute x0 -> x8, waiting for transfers between devices: none -> 163 us  [swap_near(): return lax.ppermute(array, 'dp', [(i, i ^ 2) for i in range(dp)])]
    all_gather x4 -> x3, waiting for transfers between devices: 179 us -> 27.4 us  [gather(): lax.all_gather(block, 'dp', axis=0, tiled=True, axis_index_groups=lines)]
    dot_general x29 -> x26, matrix products: 196 us -> 134 us  [dot(): lax.dot_general(left, right, (((left_dim,), (right_dim,)), ((), ())), pre...]
    pallas_call x0 -> x2, Pallas kernels: none -> 52.7 us  [expert_call(): pl.pallas_call(kernel, out_shape=outs, grid=(experts,), in_specs=[spec(ar...]
    ppermute x10, waiting for transfers between devices: 96 us -> 46.6 us  [swap_side(): return lax.ppermute(array, 'tensor', [(0, 1), (1, 0)])]
    all_gather x0 -> x1, blocking collectives: none -> 32.3 us  [gather(): lax.all_gather(block, 'dp', axis=0, tiled=True, axis_index_groups=lines)]
    unnamed x141 -> x191, local copies, waits for them, and re-layouts: 64.3 us -> 42.9 us
  transfers between devices with their start and end apart: 26 -> 33, of which waited for: 14 -> 13; matrix products, arithmetic and copies ran while one was open for 21% -> 32% of each run, Pallas kernels for 2% -> 9%
where the time goes in v2:
time: 724 us; the launch traced here: 718 us
  waiting for transfers between devices  250 us (35%)
  matrix products  134 us (19%)
  Pallas kernels  93.1 us (13%)
  local copies, waits for them, and re-layouts  88.2 us (12%)
  other arithmetic  81.6 us (11%)
  blocking collectives  32.3 us (4%)
  starting transfers between devices  22.5 us (3%)
  between operations  15.9 us (2%)
    ppermute x8, waiting for transfers between devices, swap_near(): return lax.ppermute(array, 'dp', [(i, i ^ 2) for i in range(dp)])  163 us
    dot_general x26, matrix products, dot(): lax.dot_general(left, right, (((left_dim,), (right_dim,)), ((), ())), pre...  134 us
    pallas_call x2, Pallas kernels, expert_call(): pl.pallas_call(kernel, out_shape=outs, grid=(experts,), in_specs=[spec(ar...  52.7 us
    ppermute x10, waiting for transfers between devices, swap_side(): return lax.ppermute(array, 'tensor', [(0, 1), (1, 0)])  46.6 us
    unnamed x191, local copies, waits for them, and re-layouts  42.9 us
    pallas_call x2, Pallas kernels, attend_call(): pl.pallas_call(kernel, out_shape=outs, grid=(groups,), in_specs=[spec(arr...  40.4 us
    all_gather x1, blocking collectives, gather(): lax.all_gather(block, 'dp', axis=0, tiled=True, axis_index_groups=lines)  32.3 us
    all_gather x3, waiting for transfers between devices, gather(): lax.all_gather(block, 'dp', axis=0, tiled=True, axis_index_groups=lines)  27.4 us
  transfers between devices with their start and end apart: 33, of which 13 were waited for; matrix products, arithmetic and copies ran while one was open for 32% of the time, Pallas kernels for 9%

profile of v2, /device:TPU:0, one launch (start us, length us, event | category | flops | bytes accessed | tf_op | source)
XLA Modules:
  0.0 717.7 jit_solution(14523992905213282217)
XLA Ops:
  10.6 3.0 collective-permute-start
  24.3 32.3 %all_gather.12 = bf16[256,1664]{1,0:T(8,128)(2,1)S(1)} all-gather(bf16[64,1664]{1,0:T(8,128)(2,1)S(1)} %constant_dynamic-update-slice_fusion), channel_id=1, replica_groups={{0,8,16,24},{2,10,18,26},{4,12,20,28},{6,14,22,30},{1,9,17,25},{3,11,19..., dimensions={0}, use_global_device_ids=true | all-gather | bytes 1064960 | tf_op jit(solution)/shard_map/all_gather | solution.py:255
  64.4 11.6 %collective-permute-done.1 = bf16[256,1664]{1,0:T(8,128)(2,1)S(1)} collective-permute-done((bf16[256,1664]{1,0:T(8,128)(2,1)S(1)}, bf16[256,1664]{1,0:T(8,128)(2,1)S(1)}, u32[]{:S(2)}, u32[]{:S(2)}) %collective-permute-start.1) | collective-permute-done | bytes 852000 | tf_op jit(solution)/shard_map/ppermute | solution.py:252
  77.7 6.3 collective-permute-done.3
  84.0 15.2 %fusion = (f32[1024]{0:T(1024)S(1)}, bf16[1024,1024]{1,0:T(8,128)(2,1)S(1)}) fusion(bf16[512,256]{1,0:T(8,128)(2,1)S(1)} %copy-done.42, bf16[512,256]{1,0:T(8,128)(2,1)S(1)} %copy.227, bf16[512,256]{1,0:T(8,128)(2,1)S(1)} %copy-done.46, bf16[512,256]{1,0:T(8,128)(2,1)S(1)} %copy-done.44, bf16[512,1024]{1,0:T(8,128)(2,1)} %collective-permute-done.3, pred[]{:T(512)S(6)} %eq.14), kind=kLoop, calls=%fused_computation.8 | loop fusion | flops 25164800 | bytes 4198401 | tf_op jit(solution)/shard_map/reduce_sum | solution.py:336
  99.8 2.9 convert_multiply_fusion
  109.3 19.3 %shard_map.229 = (bf16[512,1024]{1,0:T(8,128)(2,1)S(1)}, f32[4,2,1024]{2,1,0:T(2,128)S(1)}) custom-call(s32[1,1024]{1,0:T(1,128)S(1)} %subtract_subtract_fusion.begin_ref, bf16[512,1024]{1,0:T(8,128)(2,1)S(1)} %bitcast.149, bf16[256,1024]{1,0:T(8,128)(2,1)S(1)} %bitcast.151, bf16[256,1024]{1,0:T(8,128)(2,1)S(1)} %slice.592.value_ref), custom_call_target="tpu_custom_call" | custom-call | flops 2147483648 | bytes 2099200 | tf_op jit(solution)/shard_map/pallas_call | solution.py:125
  134.6 2.7 pad_maximum_fusion.4.grad_rows_ref
  138.5 27.4 %all-gather.8.cloned.1.call-done = bf16[256,4096]{1,0:T(8,128)(2,1)} async-done(((bf16[64,4096]{1,0:T(8,128)(2,1)}), bf16[256,4096]{1,0:T(8,128)(2,1)}) %all-gather.8.cloned.1.call-update) | async-done | bytes 2097168 | tf_op jit(solution)/shard_map/all_gather | solution.py:255
  167.6 3.2 constant_dynamic-update-slice_fusion.15
  176.7 3.8 collective-permute-done.8
  180.5 4.1 pad_maximum_fusion.1
  184.5 40.9 %collective-permute-done.6 = bf16[256,4096]{1,0:T(8,128)(2,1)} collective-permute-done((bf16[256,4096]{1,0:T(8,128)(2,1)}, bf16[256,4096]{1,0:T(8,128)(2,1)}, u32[]{:S(2)}, u32[]{:S(2)}) %collective-permute-start.6) | collective-permute-done | bytes 2097184 | tf_op jit(solution)/shard_map/ppermute | solution.py:252
  225.4 4.1 pad_maximum_fusion
  239.2 27.1 %collective-permute-done.10 = bf16[256,4096]{1,0:T(8,128)(2,1)} collective-permute-done((bf16[256,4096]{1,0:T(8,128)(2,1)}, bf16[256,4096]{1,0:T(8,128)(2,1)}, u32[]{:S(2)}, u32[]{:S(2)}) %collective-permute-start.10) | collective-permute-done | bytes 2097184 | tf_op jit(solution)/shard_map/ppermute | solution.py:252
  269.0 3.1 constant_dynamic-update-slice_fusion.14
  272.2 3.2 constant_dynamic-update-slice_fusion.11
  275.3 3.2 constant_dynamic-update-slice_fusion.8
  278.5 4.6 constant_dynamic-update-slice_fusion.10.up_w_ref
  283.1 4.6 constant_dynamic-update-slice_fusion.7.gate_w_ref
  287.7 25.8 %shard_map.230 = (bf16[1024,4096]{1,0:T(8,128)(2,1)S(1)}, bf16[1024,4096]{1,0:T(8,128)(2,1)}, bf16[1024,4096]{1,0:T(8,128)(2,1)}) custom-call(bf16[1024,1024]{1,0:T(8,128)(2,1)S(1)} %pad_maximum_fusion.3.rows_ref, bf16[1024,4096]{1,0:T(8,128)(2,1)} %constant_dynamic-update-slice_fusion.7.gate_w_ref, ...), custom_call_target="tpu_custom_call" | custom-call | flops 17179869184 | bytes 18907136 | tf_op jit(solution)/shard_map/pallas_call | solution.py:194
  313.6 3.3 copy-done.9
  319.4 26.9 %shard_map.231 = (bf16[1024,4096]{1,0:T(8,128)(2,1)S(1)}, bf16[1024,4096]{1,0:T(8,128)(2,1)}, f32[1024,16]{1,0:T(8,128)S(1)}) custom-call(bf16[1024,1024]{1,0:T(8,128)(2,1)S(1)} %copy-done, bf16[1024,4096]{1,0:T(8,128)(2,1)} %constant_dynamic-update-slice_fusion.13.down_w_ref, bf16[1024,4096]{1,0:T(8,128)(2,1)} %copy-done.9, ...), custom_call_target="tpu_custom_call" | custom-call | flops 8589934592 | bytes 27295744 | tf_op jit(solution)/shard_map/pallas_call | solution.py:194
  346.3 3.3 copy-done.6
  351.6 8.0 %fusion.1 = f32[512,1024]{1,0:T(8,128)} fusion(bf16[1024,4096]{1,0:T(8,128)(2,1)S(1)} %bitcast.186, bf16[1024,4096]{1,0:T(8,128)(2,1)} %get-tuple-element.36), kind=kOutput, calls=%fused_computation.15 | convolution fusion | flops 4294967296 | bytes 14680064 | tf_op jit(solution)/shard_map/dot_general | solution.py:46
  359.6 8.1 %fusion.5 = f32[512,1024]{1,0:T(8,128)} fusion(bf16[1024,4096]{1,0:T(8,128)(2,1)S(1)} %bitcast.186, bf16[1024,4096]{1,0:T(8,128)(2,1)} %get-tuple-element.36), kind=kOutput, calls=%fused_computation.19 | convolution fusion | flops 4294967296 | bytes 14680064 | tf_op jit(solution)/shard_map/dot_general | solution.py:46
  371.4 10.2 %add_convert_fusion.6 = bf16[512,1024]{1,0:T(8,128)(2,1)} fusion(f32[512,1024]{1,0:T(8,128)S(1)} %fusion.56, f32[512,1024]{1,0:T(8,128)S(1)} %copy-done.82, bf16[1024,4096]{1,0:T(8,128)(2,1)} %constant_dynamic-update-slice_fusion.7.gate_w_ref, bf16[1024,4096]{1,0:T(8,128)(2,1)} %copy-done.6), kind=kOutput, calls=%fused_computation.57 | convolution fusion | flops 4296540160 | bytes 17825792 | tf_op jit(solution)/shard_map/dot_general | solution.py:46
  383.0 10.2 %convolution_convert_fusion = bf16[512,4096]{1,0:T(8,128)(2,1)} fusion(bf16[1024,4096]{1,0:T(8,128)(2,1)} %get-tuple-element.32, bf16[512,1024]{1,0:T(8,128)(2,1)S(1)} %copy-done.25, bf16[512,1024]{1,0:T(8,128)(2,1)} %collective-permute-done.13), kind=kOutput, calls=%fused_computation.3 | convolution fusion | flops 4299161600 | bytes 14680064 | tf_op jit(solution)/shard_map/dot_general | solution.py:46
  393.4 9.6 %convolution_convert_fusion.1 = bf16[512,4096]{1,0:T(8,128)(2,1)} fusion(bf16[1024,4096]{1,0:T(8,128)(2,1)} %get-tuple-element.36, bf16[512,1024]{1,0:T(8,128)(2,1)S(1)} %copy-done.28, bf16[512,1024]{1,0:T(8,128)(2,1)S(1)} %copy-done.63), kind=kOutput, calls=%fused_computation.4 | convolution fusion | flops 4299161600 | bytes 14680064 | tf_op jit(solution)/shard_map/dot_general | solution.py:46
  403.4 6.1 convolution_convert_fusion.2
  411.5 11.3 %multiply_reduce_fusion = (f32[1024]{0:T(1024)S(1)}, f32[512]{0:T(512)S(1)}, f32[512,1024]{1,0:T(8,128)}) fusion(f32[512,1024]{1,0:T(8,128)} %copy-done.11, f32[512]{0:T(512)S(1)} %copy-done.77, f32[1024]{0:T(1024)S(1)} %get-tuple-element.127, bf16[512,1024]{1,0:T(8,128)(2,1)} %collective-permute-done.14, f32[512,1024]{1,0:T(8,128)} %fusion.57, ...), kind=kOutput, calls=%fused_computation.48 | convolution fusion | flops 4300208640 | bytes 22032384 | tf_op jit(solution)/shard_map/dot_general | solution.py:46
  422.9 4.4 multiply_convert_fusion.1
  428.2 24.4 %collective-permute-done.15 = bf16[512,1024]{1,0:T(8,128)(2,1)S(1)} collective-permute-done((bf16[512,1024]{1,0:T(8,128)(2,1)S(1)}, bf16[512,1024]{1,0:T(8,128)(2,1)S(1)}, u32[]{:S(2)}, u32[]{:S(2)}) %collective-permute-start.15) | collective-permute-done | bytes 1048608 | tf_op jit(solution)/shard_map/ppermute | solution.py:249
  455.0 9.5 %add_convert_fusion = bf16[512,4096]{1,0:T(8,128)(2,1)S(1)} fusion(bf16[512,4096]{1,0:T(8,128)(2,1)} %collective-permute-done.18, bf16[1024,4096]{1,0:T(8,128)(2,1)} %get-tuple-element.32, bf16[512,1024]{1,0:T(8,128)(2,1)S(1)} %copy-done.26, bf16[512,1024]{1,0:T(8,128)(2,1)} %collective-permute-done.13), kind=kOutput, calls=%fused_computation | convolution fusion | flops 4303355904 | bytes 18874368 | tf_op jit(solution)/shard_map/dot_general | solution.py:46
  464.5 10.2 %add_convert_fusion.1 = bf16[512,4096]{1,0:T(8,128)(2,1)} fusion(bf16[512,4096]{1,0:T(8,128)(2,1)} %collective-permute-done.17, bf16[1024,4096]{1,0:T(8,128)(2,1)} %get-tuple-element.36, bf16[512,1024]{1,0:T(8,128)(2,1)S(1)} %copy-done.29, bf16[512,1024]{1,0:T(8,128)(2,1)S(1)} %copy-done.64), kind=kOutput, calls=%fused_computation.1 | convolution fusion | flops 4303355904 | bytes 18874368 | tf_op jit(solution)/shard_map/dot_general | solution.py:46
  474.7 7.7 %add_convert_fusion.2 = bf16[512,4096]{1,0:T(8,128)(2,1)} fusion(bf16[512,4096]{1,0:T(8,128)(2,1)} %collective-permute-done.16, bf16[1024,4096]{1,0:T(8,128)(2,1)S(1)} %bitcast.154, bf16[512,1024]{1,0:T(8,128)(2,1)S(1)} %copy-done.29, bf16[512,1024]{1,0:T(8,128)(2,1)S(1)} %copy-done.64), kind=kOutput, calls=%fused_computation.2 | convolution fusion | flops 4303355904 | bytes 18874368 | tf_op jit(solution)/shard_map/dot_general | solution.py:46
  483.1 46.5 %collective-permute-done.24 = bf16[256,4096]{1,0:T(8,128)(2,1)S(1)} collective-permute-done((bf16[256,4096]{1,0:T(8,128)(2,1)S(1)}, bf16[256,4096]{1,0:T(8,128)(2,1)S(1)}, u32[]{:S(2)}, u32[]{:S(2)}) %collective-permute-start.24) | collective-permute-done | bytes 2097184 | tf_op jit(solution)/shard_map/ppermute | solution.py:252
  534.5 10.6 %fusion.27 = bf16[512,1024]{1,0:T(8,128)(2,1)} fusion(bf16[1024,4096]{1,0:T(8,128)(2,1)} %constant_dynamic-update-slice_fusion.13.down_w_ref, bf16[1024,4096]{1,0:T(8,128)(2,1)} %get-tuple-element.32), kind=kOutput, calls=%fused_computation.71 | convolution fusion | flops 4295491584 | bytes 13631488 | tf_op jit(solution)/shard_map/dot_general | solution.py:46
  548.2 21.1 %shard_map.232 = (f32[512,1024]{1,0:T(8,128)S(1)}, f32[256,1024]{1,0:T(8,128)S(1)}, f32[256,1024]{1,0:T(8,128)S(1)}) custom-call(s32[1,1024]{1,0:T(1,128)S(1)} %subtract_subtract_fusion.begin_ref, bf16[512,1024]{1,0:T(8,128)(2,1)S(1)} %bitcast.150, bf16[256,1024]{1,0:T(8,128)(2,1)S(1)} %bitcast.152, bf16[256,1024]{1,0:T(8,128)(2,1)S(1)} %copy-done.3, ...), custom_call_target="tpu_custom_call" | custom-call | flops 5368709120 | bytes 3164160 | tf_op jit(solution)/shard_map/pallas_call | solution.py:125
  573.8 8.7 %collective-permute-done.23 = bf16[256,4096]{1,0:T(8,128)(2,1)S(1)} collective-permute-done((bf16[256,4096]{1,0:T(8,128)(2,1)S(1)}, bf16[256,4096]{1,0:T(8,128)(2,1)S(1)}, u32[]{:S(2)}, u32[]{:S(2)}) %collective-permute-start.23) | collective-permute-done | bytes 2097184 | tf_op jit(solution)/shard_map/ppermute | solution.py:252
  595.1 15.8 %collective-permute-done.19 = bf16[512,1024]{1,0:T(8,128)(2,1)S(1)} collective-permute-done((bf16[512,1024]{1,0:T(8,128)(2,1)S(1)}, bf16[512,1024]{1,0:T(8,128)(2,1)S(1)}, u32[]{:S(2)}, u32[]{:S(2)}) %collective-permute-start.19) | collective-permute-done | bytes 1048608 | tf_op jit(solution)/shard_map/ppermute | solution.py:249
  610.9 2.8 multiply_reduce_fusion.1
  615.3 9.7 %collective-permute-done.22 = bf16[256,4096]{1,0:T(8,128)(2,1)} collective-permute-done((bf16[256,4096]{1,0:T(8,128)(2,1)}, bf16[256,4096]{1,0:T(8,128)(2,1)}, u32[]{:S(2)}, u32[]{:S(2)}) %collective-permute-start.22) | collective-permute-done | bytes 2097184 | tf_op jit(solution)/shard_map/ppermute | solution.py:252
  625.1 4.4 add_convert_fusion.5
  631.1 10.9 %multiply_add_fusion = f32[512,1024]{1,0:T(8,128)} fusion(f32[512,1024]{1,0:T(8,128)S(1)} %copy-done.12, bf16[512,1024]{1,0:T(8,128)(2,1)} %collective-permute-done.12, bf16[1024,4096]{1,0:T(8,128)(2,1)} %constant_dynamic-update-slice_fusion.13.down_w_ref, bf16[1024,4096]{1,0:T(8,128)(2,1)} %get-tuple-element.32), kind=kOutput, calls=%fused_computation.58 | convolution fusion | flops 4297064448 | bytes 17825792 | tf_op jit(solution)/shard_map/dot_general | solution.py:46
  655.3 15.3 %collective-permute-done.21 = bf16[256,1664]{1,0:T(8,128)(2,1)S(1)} collective-permute-done((bf16[256,1664]{1,0:T(8,128)(2,1)}, bf16[256,1664]{1,0:T(8,128)(2,1)S(1)}, u32[]{:S(2)}, u32[]{:S(2)}) %collective-permute-start.21) | collective-permute-done | bytes 852000 | tf_op jit(solution)/shard_map/ppermute | solution.py:252
  678.3 4.4 subtract_add_fusion
  691.0 12.0 %reduce-scatter.11.cloned.1.call-done = bf16[64,1664]{1,0:T(8,128)(2,1)} async-done(((bf16[256,1664]{1,0:T(8,128)(2,1)}), bf16[64,1664]{1,0:T(8,128)(2,1)}) %reduce-scatter.11.cloned.1.call-update) | async-done | bytes 213008 | tf_op jit(solution)/shard_map/reduce_scatter | solution.py:268
  (378 shorter events, 138.1 us)
Async XLA Ops:
  7.2 124.4 %all-gather.6.cloned.1.call-start = ((), (), s32[]{:S(2)}) async-start(), calls=%async_computation.5 | async-start | bytes 2621440 | tf_op jit(solution)/shard_map/all_gather | solution.py:255
  9.2 123.9 %all-gather.4.cloned.1.call-start = ((), (), s32[]{:S(2)}) async-start(), calls=%async_computation.4 | async-start | bytes 2621440 | tf_op jit(solution)/shard_map/all_gather | solution.py:255
  10.6 13.4 %collective-permute-start = (bf16[32,18]{0,1:T(8,128)(2,1)}, bf16[32,18]{0,1:T(8,128)(2,1)S(1)}, u32[]{:S(2)}, u32[]{:S(2)}) collective-permute-start(bf16[32,18]{0,1:T(8,128)(2,1)} %pad_maximum_fusion.22), channel_id=1, source_target_pairs={{0,1},{1,0},{2,3},{3,2},{4,5},{5,4},{6,7},{7,6},{8,9},{9,8},{10,11... | collective-permute-start | bytes 3464 | tf_op jit(solution)/shard_map/ppermute | solution.py:249
  15.4 150.5 %all-gather.8.cloned.1.call-start = ((), (), s32[]{:S(2)}) async-start(), calls=%async_computation.6 | async-start | bytes 2621440 | tf_op jit(solution)/shard_map/all_gather | solution.py:255
  17.5 117.1 %copy-start.24 = (bf16[512,1024]{1,0:T(8,128)(2,1)}, bf16[512,1024]{1,0:T(8,128)(2,1)S(1)}, u32[]{:S(2)}) copy-start(bf16[512,1024]{1,0:T(8,128)(2,1)S(1)} %fusion.14) | copy-start | bytes 3145732
  17.5 117.0 %collective-permute-start.13 = (bf16[512,1024]{1,0:T(8,128)(2,1)S(1)}, bf16[512,1024]{1,0:T(8,128)(2,1)}, u32[]{:S(2)}, u32[]{:S(2)}) collective-permute-start(bf16[512,1024]{1,0:T(8,128)(2,1)S(1)} %fusion.14), channel_id=1, source_target_pairs={{0,1},{1,0},{2,3},{3,2},{4,5},{5,4},{6,7},{7,6},{8,9},{9,8},{10,11... | collective-permute-start | bytes 3145736 | tf_op jit(solution)/shard_map/ppermute | solution.py:249
  21.4 62.6 %copy-start.40 = (bf16[512,256]{1,0:T(8,128)(2,1)}, bf16[512,256]{1,0:T(8,128)(2,1)S(1)}, u32[]{:S(2)}) copy-start(bf16[512,256]{1,0:T(8,128)(2,1)S(1)} %copy.227) | copy-start | bytes 786436
  56.6 19.5 %collective-permute-start.1 = (bf16[256,1664]{1,0:T(8,128)(2,1)S(1)}, bf16[256,1664]{1,0:T(8,128)(2,1)S(1)}, u32[]{:S(2)}, u32[]{:S(2)}) collective-permute-start(bf16[256,1664]{1,0:T(8,128)(2,1)S(1)} %all_gather.12), channel_id=1, source_target_pairs={{0,4},{2,6},{4,0},{6,2},{8,12},{10,14},{12,8},{14,10},{16,20},{18,... | collective-permute-start | bytes 2555912 | tf_op jit(solution)/shard_map/ppermute | solution.py:252
  60.3 23.7 %collective-permute-start.3 = (bf16[512,1024]{1,0:T(8,128)(2,1)}, bf16[512,1024]{1,0:T(8,128)(2,1)}, u32[]{:S(2)}, u32[]{:S(2)}) collective-permute-start(bf16[512,1024]{1,0:T(8,128)(2,1)} %pad_maximum_fusion.10), channel_id=1, source_target_pairs={{0,1},{1,0},{2,3},{3,2},{4,5},{5,4},{6,7},{7,6},{8,9},{9,8},{10,11... | collective-permute-start | bytes 3145736 | tf_op jit(solution)/shard_map/ppermute | solution.py:249
  63.6 609.2 %reduce-scatter.9.cloned.1.call-start = ((), (), s32[]{:S(2)}) async-start(), calls=%async_computation.9 | async-start | bytes 2621440 | tf_op jit(solution)/shard_map/reduce_scatter | solution.py:268
  76.2 23.0 %collective-permute-start.2 = (bf16[512,1664]{1,0:T(8,128)(2,1)S(1)}, bf16[512,1664]{1,0:T(8,128)(2,1)S(1)}, u32[]{:S(2)}, u32[]{:S(2)}) collective-permute-start(bf16[512,1664]{1,0:T(8,128)(2,1)S(1)} %pad_maximum_fusion.8), channel_id=1, source_target_pairs={{0,2},{2,0},{4,6},{6,4},{8,10},{10,8},{12,14},{14,12},{16,18},{18,... | collective-permute-start | bytes 5111816 | tf_op jit(solution)/shard_map/ppermute | solution.py:246
  77.5 29.8 %copy-start.35 = (f32[32,1024]{1,0:T(8,128)}, f32[32,1024]{1,0:T(8,128)S(1)}, u32[]{:S(2)}) copy-start(f32[32,1024]{1,0:T(8,128)S(1)} %get-tuple-element.177) | copy-start | bytes 393220
  99.5 29.2 %copy-start.20 = (bf16[1024,1664]{1,0:T(8,128)(2,1)}, bf16[1024,1664]{1,0:T(8,128)(2,1)S(1)}, u32[]{:S(2)}) copy-start(bf16[1024,1664]{1,0:T(8,128)(2,1)S(1)} %constant_dynamic-update-slice_fusion.4) | copy-start | bytes 10223620
  128.6 42.1 %copy-start.7 = (bf16[512,1024]{1,0:T(8,128)(2,1)}, bf16[512,1024]{1,0:T(8,128)(2,1)S(1)}, u32[]{:S(2)}) copy-start(bf16[512,1024]{1,0:T(8,128)(2,1)S(1)} %get-tuple-element.31) | copy-start | bytes 3145732
  130.4 40.4 %collective-permute-start.4 = (bf16[512,1024]{1,0:T(8,128)(2,1)}, bf16[512,1024]{1,0:T(8,128)(2,1)}, u32[]{:S(2)}, u32[]{:S(2)}) collective-permute-start(bf16[512,1024]{1,0:T(8,128)(2,1)} %convolution_convert_fusion.5), channel_id=1, source_target_pairs={{0,1},{1,0},{2,3},{3,2},{4,5},{5,4},{6,7},{7,6},{8,9},{9,8},{10,11... | collective-permute-start | bytes 3145736 | tf_op jit(solution)/shard_map/ppermute | solution.py:249
  131.6 48.9 %collective-permute-start.8 = (bf16[256,4096]{1,0:T(8,128)(2,1)}, bf16[256,4096]{1,0:T(8,128)(2,1)}, u32[]{:S(2)}, u32[]{:S(2)}) collective-permute-start(bf16[256,4096]{1,0:T(8,128)(2,1)} %all-gather.6.cloned.1.call-done), channel_id=1, source_target_pairs={{0,4},{2,6},{4,0},{6,2},{8,12},{10,14},{12,8},{14,10},{16,20},{18,... | collective-permute-start | bytes 6291464 | tf_op jit(solution)/shard_map/ppermute | solution.py:252
  133.1 92.3 %collective-permute-start.6 = (bf16[256,4096]{1,0:T(8,128)(2,1)}, bf16[256,4096]{1,0:T(8,128)(2,1)}, u32[]{:S(2)}, u32[]{:S(2)}) collective-permute-start(bf16[256,4096]{1,0:T(8,128)(2,1)} %all-gather.4.cloned.1.call-done), channel_id=1, source_target_pairs={{0,4},{2,6},{4,0},{6,2},{8,12},{10,14},{12,8},{14,10},{16,20},{18,... | collective-permute-start | bytes 6291464 | tf_op jit(solution)/shard_map/ppermute | solution.py:252
  138.5 32.2 %copy-start.41 = (bf16[512,256]{1,0:T(8,128)(2,1)S(1)}, bf16[512,256]{1,0:T(8,128)(2,1)}, u32[]{:S(2)}) copy-start(bf16[512,256]{1,0:T(8,128)(2,1)} %copy-done.40) | copy-start | bytes 786436
  138.5 32.2 %copy-start.43 = (bf16[512,256]{1,0:T(8,128)(2,1)S(1)}, bf16[512,256]{1,0:T(8,128)(2,1)}, u32[]{:S(2)}) copy-start(bf16[512,256]{1,0:T(8,128)(2,1)} %copy.228) | copy-start | bytes 786436
  138.5 32.2 %copy-start.45 = (bf16[512,256]{1,0:T(8,128)(2,1)S(1)}, bf16[512,256]{1,0:T(8,128)(2,1)}, u32[]{:S(2)}) copy-start(bf16[512,256]{1,0:T(8,128)(2,1)} %copy.225) | copy-start | bytes 786436
  138.5 32.2 %copy-start.47 = (bf16[512,256]{1,0:T(8,128)(2,1)S(1)}, bf16[512,256]{1,0:T(8,128)(2,1)}, u32[]{:S(2)}) copy-start(bf16[512,256]{1,0:T(8,128)(2,1)} %copy.226) | copy-start | bytes 786436
  165.9 100.3 %collective-permute-start.10 = (bf16[256,4096]{1,0:T(8,128)(2,1)}, bf16[256,4096]{1,0:T(8,128)(2,1)}, u32[]{:S(2)}, u32[]{:S(2)}) collective-permute-start(bf16[256,4096]{1,0:T(8,128)(2,1)} %all-gather.8.cloned.1.call-done), channel_id=1, source_target_pairs={{0,4},{2,6},{4,0},{6,2},{8,12},{10,14},{12,8},{14,10},{16,20},{18,... | collective-permute-start | bytes 6291464 | tf_op jit(solution)/shard_map/ppermute | solution.py:252
  174.9 57.6 %copy-start.27 = (bf16[512,1024]{1,0:T(8,128)(2,1)}, bf16[512,1024]{1,0:T(8,128)(2,1)S(1)}, u32[]{:S(2)}) copy-start(bf16[512,1024]{1,0:T(8,128)(2,1)S(1)} %multiply_convert_fusion.2) | copy-start | bytes 3145732
  174.9 50.5 %copy-start.16 = (bf16[256,4096]{1,0:T(8,128)(2,1)S(1)}, bf16[256,4096]{1,0:T(8,128)(2,1)}, u32[]{:S(2)}) copy-start(bf16[256,4096]{1,0:T(8,128)(2,1)} %all-gather.4.cloned.1.call-done) | copy-start | bytes 6291460
  175.0 57.6 %collective-permute-start.5 = (bf16[512,1024]{1,0:T(8,128)(2,1)S(1)}, bf16[512,1024]{1,0:T(8,128)(2,1)S(1)}, u32[]{:S(2)}, u32[]{:S(2)}) collective-permute-start(bf16[512,1024]{1,0:T(8,128)(2,1)S(1)} %multiply_convert_fusion.2), channel_id=1, source_target_pairs={{0,1},{1,0},{2,3},{3,2},{4,5},{5,4},{6,7},{7,6},{8,9},{9,8},{10,11... | collective-permute-start | bytes 3145736 | tf_op jit(solution)/shard_map/ppermute | solution.py:249
  184.5 93.9 %collective-permute-start.9 = (bf16[512,4096]{1,0:T(8,128)(2,1)}, bf16[512,4096]{1,0:T(8,128)(2,1)}, u32[]{:S(2)}, u32[]{:S(2)}) collective-permute-start(bf16[512,4096]{1,0:T(8,128)(2,1)} %pad_maximum_fusion.1), channel_id=1, source_target_pairs={{0,2},{2,0},{4,6},{6,4},{8,10},{10,8},{12,14},{14,12},{16,18},{18,... | collective-permute-start | bytes 12582920 | tf_op jit(solution)/shard_map/ppermute | solution.py:246
  229.5 53.6 %collective-permute-start.7 = (bf16[512,4096]{1,0:T(8,128)(2,1)}, bf16[512,4096]{1,0:T(8,128)(2,1)}, u32[]{:S(2)}, u32[]{:S(2)}) collective-permute-start(bf16[512,4096]{1,0:T(8,128)(2,1)} %pad_maximum_fusion), channel_id=1, source_target_pairs={{0,2},{2,0},{4,6},{6,4},{8,10},{10,8},{12,14},{14,12},{16,18},{18,... | collective-permute-start | bytes 12582920 | tf_op jit(solution)/shard_map/ppermute | solution.py:246
  268.9 47.9 %collective-permute-start.11 = (bf16[512,4096]{1,0:T(8,128)(2,1)S(1)}, bf16[512,4096]{1,0:T(8,128)(2,1)S(1)}, u32[]{:S(2)}, u32[]{:S(2)}) collective-permute-start(bf16[512,4096]{1,0:T(8,128)(2,1)S(1)} %pad_maximum_fusion.2), channel_id=1, source_target_pairs={{0,2},{2,0},{4,6},{6,4},{8,10},{10,8},{12,14},{14,12},{16,18},{18,... | collective-permute-start | bytes 12582920 | tf_op jit(solution)/shard_map/ppermute | solution.py:246
  319.4 32.2 %slice-start.3 = ((s8[8388608]{0:T(1024)(128)(4,1)}), s8[4194304]{0:T(1024)(128)(4,1)S(1)}, s32[]{:S(2)}) async-start(s8[8388608]{0:T(1024)(128)(4,1)} %bitcast.185), calls=%async_computation.14 | async-start | bytes 8388608
  319.4 32.2 %slice-start.4 = ((s8[8388608]{0:T(1024)(128)(4,1)}), s8[4194304]{0:T(1024)(128)(4,1)S(1)}, s32[]{:S(2)}) async-start(s8[8388608]{0:T(1024)(128)(4,1)} %bitcast.185), calls=%async_computation.15 | async-start | bytes 8388608
  381.6 29.8 %collective-permute-start.14 = (bf16[512,1024]{1,0:T(8,128)(2,1)}, bf16[512,1024]{1,0:T(8,128)(2,1)}, u32[]{:S(2)}, u32[]{:S(2)}) collective-permute-start(bf16[512,1024]{1,0:T(8,128)(2,1)} %add_convert_fusion.6), channel_id=1, source_target_pairs={{0,1},{1,0},{2,3},{3,2},{4,5},{5,4},{6,7},{7,6},{8,9},{9,8},{10,11... | collective-permute-start | bytes 3145736 | tf_op jit(solution)/shard_map/ppermute | solution.py:249
  393.2 61.8 %collective-permute-start.18 = (bf16[512,4096]{1,0:T(8,128)(2,1)}, bf16[512,4096]{1,0:T(8,128)(2,1)}, u32[]{:S(2)}, u32[]{:S(2)}) collective-permute-start(bf16[512,4096]{1,0:T(8,128)(2,1)} %convolution_convert_fusion), channel_id=1, source_target_pairs={{0,2},{2,0},{4,6},{6,4},{8,10},{10,8},{12,14},{14,12},{16,18},{18,... | collective-permute-start | bytes 12582920 | tf_op jit(solution)/shard_map/ppermute | solution.py:246
  403.1 61.4 %collective-permute-start.17 = (bf16[512,4096]{1,0:T(8,128)(2,1)}, bf16[512,4096]{1,0:T(8,128)(2,1)}, u32[]{:S(2)}, u32[]{:S(2)}) collective-permute-start(bf16[512,4096]{1,0:T(8,128)(2,1)} %convolution_convert_fusion.1), channel_id=1, source_target_pairs={{0,2},{2,0},{4,6},{6,4},{8,10},{10,8},{12,14},{14,12},{16,18},{18,... | collective-permute-start | bytes 12582920 | tf_op jit(solution)/shard_map/ppermute | solution.py:246
  409.5 65.2 %collective-permute-start.16 = (bf16[512,4096]{1,0:T(8,128)(2,1)}, bf16[512,4096]{1,0:T(8,128)(2,1)}, u32[]{:S(2)}, u32[]{:S(2)}) collective-permute-start(bf16[512,4096]{1,0:T(8,128)(2,1)} %convolution_convert_fusion.2), channel_id=1, source_target_pairs={{0,2},{2,0},{4,6},{6,4},{8,10},{10,8},{12,14},{14,12},{16,18},{18,... | collective-permute-start | bytes 12582920 | tf_op jit(solution)/shard_map/ppermute | solution.py:246
  427.3 27.7 %copy-start.26 = (bf16[512,1024]{1,0:T(8,128)(2,1)S(1)}, bf16[512,1024]{1,0:T(8,128)(2,1)}, u32[]{:S(2)}) copy-start(bf16[512,1024]{1,0:T(8,128)(2,1)} %copy-done.24) | copy-start | bytes 3145732
  427.3 25.3 %collective-permute-start.15 = (bf16[512,1024]{1,0:T(8,128)(2,1)S(1)}, bf16[512,1024]{1,0:T(8,128)(2,1)S(1)}, u32[]{:S(2)}, u32[]{:S(2)}) collective-permute-start(bf16[512,1024]{1,0:T(8,128)(2,1)S(1)} %get-tuple-element.131), channel_id=1, source_target_pairs={{0,1},{1,0},{2,3},{3,2},{4,5},{5,4},{6,7},{7,6},{8,9},{9,8},{10,11... | collective-permute-start | bytes 3145736 | tf_op jit(solution)/shard_map/ppermute | solution.py:249
  482.6 47.1 %collective-permute-start.24 = (bf16[256,4096]{1,0:T(8,128)(2,1)S(1)}, bf16[256,4096]{1,0:T(8,128)(2,1)S(1)}, u32[]{:S(2)}, u32[]{:S(2)}) collective-permute-start(bf16[256,4096]{1,0:T(8,128)(2,1)S(1)} %slice.330), channel_id=1, source_target_pairs={{0,4},{2,6},{4,0},{6,2},{8,12},{10,14},{12,8},{14,10},{16,20},{18,... | collective-permute-start | bytes 6291464 | tf_op jit(solution)/shard_map/ppermute | solution.py:252
  531.8 143.1 %reduce-scatter.7.cloned.1.call-start = ((), (), s32[]{:S(2)}) async-start(), calls=%async_computation.8 | async-start | bytes 2621440 | tf_op jit(solution)/shard_map/reduce_scatter | solution.py:268
  533.9 48.6 %collective-permute-start.23 = (bf16[256,4096]{1,0:T(8,128)(2,1)S(1)}, bf16[256,4096]{1,0:T(8,128)(2,1)S(1)}, u32[]{:S(2)}, u32[]{:S(2)}) collective-permute-start(bf16[256,4096]{1,0:T(8,128)(2,1)S(1)} %slice.328), channel_id=1, source_target_pairs={{0,4},{2,6},{4,0},{6,2},{8,12},{10,14},{12,8},{14,10},{16,20},{18,... | collective-permute-start | bytes 6291464 | tf_op jit(solution)/shard_map/ppermute | solution.py:252
  545.0 84.8 %collective-permute-start.12 = (bf16[512,1024]{1,0:T(8,128)(2,1)}, bf16[512,1024]{1,0:T(8,128)(2,1)}, u32[]{:S(2)}, u32[]{:S(2)}) collective-permute-start(bf16[512,1024]{1,0:T(8,128)(2,1)} %fusion.27), channel_id=1, source_target_pairs={{0,1},{1,0},{2,3},{3,2},{4,5},{5,4},{6,7},{7,6},{8,9},{9,8},{10,11... | collective-permute-start | bytes 3145736 | tf_op jit(solution)/shard_map/ppermute | solution.py:249
  548.2 24.7 %copy-start.36 = (f32[32,1024]{1,0:T(8,128)S(1)}, f32[32,1024]{1,0:T(8,128)}, u32[]{:S(2)}) copy-start(f32[32,1024]{1,0:T(8,128)} %copy-done.35) | copy-start | bytes 393220
  571.4 53.7 %collective-permute-start.22 = (bf16[256,4096]{1,0:T(8,128)(2,1)}, bf16[256,4096]{1,0:T(8,128)(2,1)}, u32[]{:S(2)}, u32[]{:S(2)}) collective-permute-start(bf16[256,4096]{1,0:T(8,128)(2,1)} %slice.326), channel_id=1, source_target_pairs={{0,4},{2,6},{4,0},{6,2},{8,12},{10,14},{12,8},{14,10},{16,20},{18,... | collective-permute-start | bytes 6291464 | tf_op jit(solution)/shard_map/ppermute | solution.py:252
  584.7 92.5 %reduce-scatter.5.cloned.1.call-start = ((), (), s32[]{:S(2)}) async-start(), calls=%async_computation.7 | async-start | bytes 2621440 | tf_op jit(solution)/shard_map/reduce_scatter | solution.py:268
  590.7 20.3 %collective-permute-start.19 = (bf16[512,1024]{1,0:T(8,128)(2,1)S(1)}, bf16[512,1024]{1,0:T(8,128)(2,1)S(1)}, u32[]{:S(2)}, u32[]{:S(2)}) collective-permute-start(bf16[512,1024]{1,0:T(8,128)(2,1)S(1)} %get-tuple-element.183), channel_id=1, source_target_pairs={{0,1},{1,0},{2,3},{3,2},{4,5},{5,4},{6,7},{7,6},{8,9},{9,8},{10,11... | collective-permute-start | bytes 3145736 | tf_op jit(solution)/shard_map/ppermute | solution.py:249
  615.3 33.5 %collective-permute-start.20 = (bf16[512,1664]{1,0:T(8,128)(2,1)}, bf16[512,1664]{1,0:T(8,128)(2,1)}, u32[]{:S(2)}, u32[]{:S(2)}) collective-permute-start(bf16[512,1664]{1,0:T(8,128)(2,1)} %pad_maximum_fusion.9), channel_id=1, source_target_pairs={{0,2},{2,0},{4,6},{6,4},{8,10},{10,8},{12,14},{14,12},{16,18},{18,... | collective-permute-start | bytes 5111816 | tf_op jit(solution)/shard_map/ppermute | solution.py:246
  629.5 73.6 %reduce-scatter.11.cloned.1.call-start = ((), (), s32[]{:S(2)}) async-start(), calls=%async_computation.10 | async-start | bytes 1064960 | tf_op jit(solution)/shard_map/reduce_scatter | solution.py:268
  651.9 18.6 %collective-permute-start.21 = (bf16[256,1664]{1,0:T(8,128)(2,1)}, bf16[256,1664]{1,0:T(8,128)(2,1)S(1)}, u32[]{:S(2)}, u32[]{:S(2)}) collective-permute-start(bf16[256,1664]{1,0:T(8,128)(2,1)} %slice.398), channel_id=1, source_target_pairs={{0,4},{2,6},{4,0},{6,2},{8,12},{10,14},{12,8},{14,10},{16,20},{18,... | collective-permute-start | bytes 2555912 | tf_op jit(solution)/shard_map/ppermute | solution.py:252
  704.7 4.4 collective-permute-start.25
  (73 other events, 391.1 us)
Sparse Core Ops, SparseCore 0:
  10.2 62.2 all-gather.5
  74.6 44.7 all-gather.3
  121.5 44.4 all-gather.7
  531.9 44.2 reduce-scatter.8
  584.8 44.2 reduce-scatter.6
  631.2 43.1 reduce-scatter.4
  678.4 24.6 reduce-scatter.10
